TPU v7x, 32 devices: a whole 2x2x4 slice. The times are simulated.
32 devices in a mesh: group: 2 (over y), seq: 8 (over z, x), tensor: 2 (over core).
Axes of the slice: x: 2, y: 2, z: 4, core: 2. Of those that a mesh axis runs over, the one named last changes fastest.
Arguments:
- streams: bfloat16 [3, 128, 16, 2048], P(None, 'seq', 'group', 'tensor'), parts along dimension 2, may hold values from -6 to 6
- short_taps: float32 [3, 3, 2048], P(None, None, 'tensor'), may hold values from -3 to 3
- long_filters: bfloat16 [2, 128, 8, 2048], P(None, 'seq', None, 'tensor'), may hold values from -0.1875 to 0.1875
- out_grad: bfloat16 [128, 16, 2048], P('seq', 'group', 'tensor'), parts along dimension 1, may hold values from -6 to 6
Outputs:
- layer_out: bfloat16 [128, 16, 2048], P('seq', 'group', 'tensor'), parts along dimension 1
- stream_grads: bfloat16 [3, 128, 16, 2048], P(None, 'seq', 'group', 'tensor'), parts along dimension 2
- tap_grads: float32 [6, 3, 2048], P('group', None, 'tensor'), parts along dimension 0
There are 2 independent parts, one for each index of `group`. A program takes and returns all parts, laid end to end along the dimension named above; an argument that names none is the same for every part. Nothing has to cross between parts.
All inputs are finite; a program needn't handle non-finite values.
Results may differ from a plain program's by a relative error of at most 0.0064.
Values may be sent and summed in bfloat16 or wider, within the bound.
No kernel may reach another device: no remote copies, remote signals or barrier semaphores. Data moves between devices by JAX's collectives and lax.ppermute only.
A program may use at most 64 MiB of HBM per device.

v0:
```python
import functools
import math

import jax
import jax.numpy as jnp
import numpy as np
from jax import lax
from jax.experimental import pallas as pl
from jax.experimental.pallas import tpu as pltpu
from jax.sharding import PartitionSpec as P

HIGHEST_PRECISION = lax.Precision.HIGHEST
BF16 = jnp.bfloat16
F32 = jnp.float32
LANES = 128
TAPS = 3
TAP_ROWS = 16
CHUNK = 16
VMEM_LIMIT = 40 * 1024 * 1024


def split_bf16(value):
    high = value.astype(BF16)
    return high, (value - high.astype(F32)).astype(BF16)


def odd_transform(parts):
    count = len(parts)
    if count == 1:
        return [(parts[0], None)]
    even = odd_transform(parts[0::2])
    odd = odd_transform(parts[1::2])
    low, high = [], []
    for j in range(count // 2):
        angle = math.pi * (2 * j + 1) / (2 * count)
        cos, sin = math.cos(angle), math.sin(angle)
        even_real, even_imag = even[j]
        odd_real, odd_imag = odd[j]
        if odd_imag is None:
            turn_real, turn_imag = odd_real * cos, odd_real * -sin
            low.append((even_real + turn_real, turn_imag))
            high.append((even_real - turn_real, turn_imag))
        else:
            turn_real = odd_real * cos + odd_imag * sin
            turn_imag = odd_imag * cos - odd_real * sin
            low.append((even_real + turn_real, even_imag + turn_imag))
            high.append((even_real - turn_real, turn_imag - even_imag))
    return low + high[::-1]


def odd_transform_back(slots):
    count = len(slots)
    if count == 1:
        return [slots[0][0]]
    even, odd = [], []
    for j in range(count // 2):
        angle = math.pi * (2 * j + 1) / (2 * count)
        cos, sin = math.cos(angle), math.sin(angle)
        low_real, low_imag = slots[j]
        high_real, high_imag = slots[count - 1 - j]
        diff_real = low_real - high_real
        sum_imag = low_imag + high_imag
        if count == 2:
            even.append((low_real + high_real, None))
            odd.append((diff_real * cos - sum_imag * sin, None))
        else:
            even.append((low_real + high_real, low_imag - high_imag))
            odd.append((diff_real * cos - sum_imag * sin, sum_imag * cos + diff_real * sin))
    even_out = odd_transform_back(even)
    odd_out = odd_transform_back(odd)
    return [part for pair in zip(even_out, odd_out) for part in pair]


def transform_tables(blocks, rows):
    length = blocks * rows
    slot = np.arange(blocks)[:, None, None]
    freq = np.arange(rows)[None, :, None]
    pos = np.arange(rows)[None, None, :]
    number = ((2 * slot + 1 + 4 * blocks * freq) * pos) % (4 * length)
    angle = number * (np.pi / (2 * length))
    cos, sin = np.cos(angle), np.sin(angle)
    forward = np.concatenate(
        [np.concatenate([cos, sin], axis=2), np.concatenate([-sin, cos], axis=2)], axis=1
    )
    back = np.swapaxes(forward, 1, 2) / length

    def halves(table):
        high = table.astype(BF16)
        low = (table - high.astype(np.float64)).astype(BF16)
        return np.concatenate([high, low], axis=1)

    return halves(forward), halves(back)


def shift_blocks(edge, blocks, by):
    rolled = pltpu.roll(edge, by % edge.shape[0], 0)
    block = lax.broadcasted_iota(jnp.int32, edge.shape, 0) % blocks
    empty = 0 if by > 0 else blocks - 1
    return jnp.where(block == empty, 0.0, rolled)


def pack_kernel(me_ref, streams_ref, filters_ref, grad_ref, *refs):
    outs, sems = refs[:-1], refs[-1]
    slab = grad_ref.shape[0]
    me = me_ref[0]
    copies = []
    for k, (by, out) in enumerate(zip(sending_order(len(outs)), outs)):
        lanes = pl.ds(pl.multiple_of((me ^ by) * LANES, LANES), LANES)
        at = 0
        for part, source in enumerate((streams_ref, filters_ref, grad_ref)):
            size = source.shape[0]
            copies.append(
                pltpu.make_async_copy(
                    source.at[:, lanes], out.at[pl.ds(at, size)], sems.at[k, part]
                )
            )
            at += size
    for copy in copies:
        copy.start()
    for copy in copies:
        copy.wait()


def tables_kernel(me_ref, packed_ref, taps_ref, forward_ref, back_ref, *refs):
    del packed_ref
    outs, sems = refs[:-1], refs[-1]
    lanes = pl.ds(pl.multiple_of(me_ref[0] * LANES, LANES), LANES)
    sources = (taps_ref.at[:, :, lanes], forward_ref, back_ref)
    copies = [
        pltpu.make_async_copy(source, out, sems.at[n])
        for n, (source, out) in enumerate(zip(sources, outs))
    ]
    for copy in copies:
        copy.start()
    for copy in copies:
        copy.wait()


def core_kernel(blocks, partners, me_ref, *refs):
    msgs = refs[:partners]
    weights, fwd_ref, back_ref = refs[partners : partners + 3]
    outs = refs[partners + 3 : 2 * partners + 3]
    scratch = refs[2 * partners + 3 :]
    raw, sig, gate, grad, zh, zl, spec, turned, cot, conv, grads = scratch
    me = me_ref[0]
    total = sig.shape[1]
    rows = total // blocks
    slab = total // partners
    halo = (TAPS - 1) * blocks

    def weight(stream, tap):
        return weights[stream, tap : tap + 1]

    for k, by in enumerate(sending_order(partners)):
        start = pl.multiple_of((me ^ by) * slab, slab)
        for s in range(3):
            raw[s, pl.ds(halo + start, slab)] = msgs[k][s * slab : (s + 1) * slab].astype(F32)
        sig[2, pl.ds(start, slab)] = msgs[k][3 * slab : 4 * slab].astype(F32)
        sig[3, pl.ds(start, slab)] = msgs[k][4 * slab : 5 * slab].astype(F32)
        grad[pl.ds(start, slab)] = msgs[k][5 * slab : 6 * slab].astype(F32)
    for s in range(3):
        raw[s, 0:halo] = shift_blocks(raw[s, total : total + halo], blocks, 1)

    @pl.loop(0, total // slab)
    def _(step):
        base = pl.multiple_of(step * slab, slab)

        def filtered(s):
            now = raw[s, pl.ds(base + 2 * blocks, slab)]
            prev_one = raw[s, pl.ds(base + blocks, slab)]
            prev_two = raw[s, pl.ds(base, slab)]
            both = weight(s, 0) * now + weight(s, 1) * prev_one + weight(s, 2) * prev_two
            return both.astype(BF16).astype(F32)

        sig[0, pl.ds(base, slab)] = filtered(0)
        gate[pl.ds(base, slab)] = filtered(1)
        sig[1, pl.ds(base, slab)] = filtered(2) * grad[pl.ds(base, slab)]

    def store_slots(parts, row, col):
        for j, (real, imag) in enumerate(odd_transform(parts)):
            for at, value in ((row, real), (rows + row, imag)):
                high, low = split_bf16(value)
                zh[j, pl.ds(at, CHUNK), col : col + LANES] = high
                zl[j, pl.ds(at, CHUNK), col : col + LANES] = low

    def times(table, j, high, low):
        size = 2 * rows
        main = jnp.dot(table[j, 0:size], high, preferred_element_type=F32)
        main += jnp.dot(table[j, 0:size], low, preferred_element_type=F32)
        return main + jnp.dot(table[j, size : 2 * size], high, preferred_element_type=F32)

    @pl.loop(0, rows // CHUNK)
    def _(step):
        row = pl.multiple_of(step * CHUNK, CHUNK)
        for s in range(4):
            parts = [
                sig[s, pl.ds(row * blocks + b, CHUNK, stride=blocks)] for b in range(blocks)
            ]
            store_slots(parts, row, s * LANES)

    def products(data, first, second):
        real, imag = data[:rows], data[rows:]
        a_real, a_imag = real[:, :LANES], imag[:, :LANES]
        c_real, c_imag = real[:, LANES:], imag[:, LANES:]
        (f_real, f_imag), (s_real, s_imag) = first, second
        left = jnp.concatenate(
            [a_real * f_real - a_imag * f_imag, a_real * f_imag + a_imag * f_real], axis=0
        )
        right = jnp.concatenate(
            [c_real * s_real + c_imag * s_imag, c_imag * s_real - c_real * s_imag], axis=0
        )
        return jnp.concatenate([left, right], axis=1)

    def filter_spec(j, f):
        cols = slice(f * LANES, (f + 1) * LANES)
        return spec[j, 0:rows, cols], spec[j, rows : 2 * rows, cols]

    @pl.loop(0, blocks, unroll=blocks)
    def _(j):
        data = times(fwd_ref, j, zh[j], zl[j])
        spec[j] = data[:, 2 * LANES :]
        high, low = split_bf16(
            products(data[:, : 2 * LANES], filter_spec(j, 0), filter_spec(j, 1))
        )
        turned[j] = times(back_ref, j, high, low)

    def blocks_of(row, col):
        return odd_transform_back(
            [
                (
                    turned[j, pl.ds(row, CHUNK), col : col + LANES],
                    turned[j, pl.ds(rows + row, CHUNK), col : col + LANES],
                )
                for j in range(blocks)
            ]
        )

    @pl.loop(0, rows // CHUNK)
    def _(step):
        row = pl.multiple_of(step * CHUNK, CHUNK)
        first = blocks_of(row, 0)
        gated_grad = blocks_of(row, LANES)
        forward, backward = [], []
        for b in range(blocks):
            place = pl.ds(row * blocks + b, CHUNK, stride=blocks)
            gate_one = gate[place]
            cot[1, place] = (gated_grad[b] * first[b]).astype(BF16).astype(F32)
            forward.append(gate_one * first[b])
            backward.append(gate_one * gated_grad[b])
        store_slots(forward, row, 0)
        store_slots(backward, row, LANES)

    @pl.loop(0, blocks, unroll=blocks)
    def _(j):
        data = times(fwd_ref, j, zh[j, :, : 2 * LANES], zl[j, :, : 2 * LANES])
        high, low = split_bf16(products(data, filter_spec(j, 1), filter_spec(j, 0)))
        turned[j] = times(back_ref, j, high, low)

    @pl.loop(0, rows // CHUNK)
    def _(step):
        row = pl.multiple_of(step * CHUNK, CHUNK)
        second = blocks_of(row, 0)
        value_grad = blocks_of(row, LANES)
        for b in range(blocks):
            place = pl.ds(row * blocks + b, CHUNK, stride=blocks)
            conv[place] = second[b]
            cot[0, place] = value_grad[b].astype(BF16).astype(F32)

    for s in range(2):
        cot[s, total : total + halo] = shift_blocks(cot[s, 0:halo], blocks, -1)

    def finish(step, sums):
        base = pl.multiple_of(step * slab, slab)
        here = [cot[s, pl.ds(base, slab)] for s in range(2)]
        last = (grad[pl.ds(base, slab)] * conv[pl.ds(base, slab)]).astype(BF16).astype(F32)
        cot[2, pl.ds(base, slab)] = last
        here.append(last)
        for s in range(2):
            next_one = cot[s, pl.ds(base + blocks, slab)]
            next_two = cot[s, pl.ds(base + 2 * blocks, slab)]
            grads[s, pl.ds(base, slab)] = (
                weight(s, 0) * here[s] + weight(s, 1) * next_one + weight(s, 2) * next_two
            ).astype(BF16)
        added = []
        for s in range(3):
            for tap in range(TAPS):
                term = here[s] * raw[s, pl.ds(base + (TAPS - 1 - tap) * blocks, slab)]
                added.append(jnp.sum(term.reshape(slab // 8, 8, LANES), axis=0))
        return tuple(a + b for a, b in zip(sums, added))

    zeros = tuple(jnp.zeros((8, LANES), F32) for _ in range(3 * TAPS))
    sums = lax.fori_loop(0, total // slab, finish, zeros)
    cot[2, total : total + halo] = shift_blocks(cot[2, 0:halo], blocks, -1)
    scale = 1.0 / math.sqrt(total)
    tap_rows = [jnp.sum(part, axis=0, keepdims=True) * scale for part in sums]
    pad = jnp.zeros((TAP_ROWS - 3 * TAPS, LANES), F32)
    tap_block = jnp.concatenate(tap_rows + [pad], axis=0).astype(BF16)
    for k, by in enumerate(sending_order(partners)):
        start = pl.multiple_of((me ^ by) * slab, slab)
        outs[k][0:slab] = conv[pl.ds(start, slab)].astype(BF16)
        for s in range(2):
            at = (s + 1) * slab
            outs[k][at : at + slab] = grads[s, pl.ds(start, slab)]
        at = 3 * slab
        now, prev_one, prev_two = (raw[2, pl.ds(start + j * blocks, halo)] for j in (2, 1, 0))
        gate_two = weight(2, 0) * now + weight(2, 1) * prev_one + weight(2, 2) * prev_two
        first = gate_two.astype(BF16).astype(F32) * conv[pl.ds(start, halo)]
        outs[k][at : at + halo] = first.astype(BF16)
        at += halo
        begin = start + slab - halo
        now, next_one, next_two = (cot[2, pl.ds(begin + j * blocks, halo)] for j in range(TAPS))
        end = weight(2, 0) * now + weight(2, 1) * next_one + weight(2, 2) * next_two
        outs[k][at : at + halo] = end.astype(BF16)
        at += halo
        outs[k][at:] = tap_block


def home_kernel(blocks, partners, me_ref, *refs):
    msgs = refs[:partners]
    stream_ref, grad_ref, taps_ref = refs[partners : partners + 3]
    layer_ref, grads_ref, tap_ref = refs[partners + 3 :]
    me = me_ref[0]
    slab = stream_ref.shape[0]
    halo = (TAPS - 1) * blocks
    rest = slab - halo
    for k, by in enumerate(sending_order(partners)):
        lanes = pl.ds(pl.multiple_of((me ^ by) * LANES, LANES), LANES)
        msg = msgs[k]
        conv = msg[0:slab].astype(F32)
        tap = [taps_ref[2, j : j + 1, lanes] for j in range(TAPS)]
        stream = stream_ref[:, lanes].astype(F32)
        gate = tap[0] * stream[halo:] + tap[1] * stream[blocks : blocks + rest]
        gate = (gate + tap[2] * stream[:rest]).astype(BF16).astype(F32)
        layer_ref[0:halo, lanes] = msg[3 * slab : 3 * slab + halo]
        layer_ref[halo:slab, lanes] = (gate * conv[halo:]).astype(BF16)
        cot = (grad_ref[:, lanes].astype(F32) * conv).astype(BF16).astype(F32)
        last = tap[0] * cot[:rest] + tap[1] * cot[blocks : blocks + rest] + tap[2] * cot[halo:]
        grads_ref[0 : 2 * slab, lanes] = msg[slab : 3 * slab]
        grads_ref[2 * slab : 3 * slab - halo, lanes] = last.astype(BF16)
        grads_ref[3 * slab - halo : 3 * slab, lanes] = msg[3 * slab + halo : 3 * slab + 2 * halo]
        block = msg[3 * slab + 2 * halo :].astype(F32)
        for s in range(3):
            tap_ref[s, :, lanes] = block[s * TAPS : (s + 1) * TAPS]


def sending_order(count):
    far = [k for k in range(1, count) if k > 2]
    return [0] + far + [k for k in (2, 1) if k < count]


def traded(messages, count):
    out = [messages[0]]
    for k, message in zip(sending_order(count)[1:], messages[1:]):
        out.append(lax.ppermute(message, "seq", [(i, i ^ k) for i in range(count)]))
    return out


def whole_specs(count):
    return [pl.BlockSpec(memory_space=pltpu.VMEM) for _ in range(count)]


def in_hbm(array):
    return pltpu.with_memory_space_constraint(array, pltpu.HBM)


def shape(*dims, dtype=BF16):
    return jax.ShapeDtypeStruct(dims, dtype)


def core_call(place, arrived, tables, blocks):
    count = len(arrived)
    slab = arrived[0].shape[0] // 6
    total = slab * count
    rows = total // blocks
    halo = (TAPS - 1) * blocks
    scalar = pl.BlockSpec(memory_space=pltpu.SMEM)
    params = pltpu.CompilerParams(vmem_limit_bytes=VMEM_LIMIT)
    answer_rows = 3 * slab + 2 * halo + TAP_ROWS
    return pl.pallas_call(
        functools.partial(core_kernel, blocks, count),
        out_shape=[shape(answer_rows, LANES)] * count,
        in_specs=[scalar] + whole_specs(count + 3),
        out_specs=whole_specs(count),
        scratch_shapes=[
            pltpu.VMEM((3, halo + total, LANES), F32),
            pltpu.VMEM((4, total, LANES), F32),
            pltpu.VMEM((total, LANES), F32),
            pltpu.VMEM((total, LANES), F32),
            pltpu.VMEM((blocks, 2 * rows, 4 * LANES), BF16),
            pltpu.VMEM((blocks, 2 * rows, 4 * LANES), BF16),
            pltpu.VMEM((blocks, 2 * rows, 2 * LANES), F32),
            pltpu.VMEM((blocks, 2 * rows, 2 * LANES), F32),
            pltpu.VMEM((3, total + halo, LANES), F32),
            pltpu.VMEM((total, LANES), F32),
            pltpu.VMEM((2, total, LANES), BF16),
        ],
        compiler_params=params,
        name="core",
    )(place, *arrived, *tables)


def short_local(streams, short_taps, long_filters, out_grad):
    count = lax.axis_size("seq")
    me = lax.axis_index("seq").astype(jnp.int32)
    place = me[None]
    _, local_rows, blocks, channels = streams.shape
    slab = local_rows * blocks
    flat_streams = streams.reshape(3 * slab, channels)
    flat_filters = long_filters.reshape(2 * slab, channels)
    flat_grad = out_grad.reshape(slab, channels)
    scalar = pl.BlockSpec(memory_space=pltpu.SMEM)
    anywhere = pl.BlockSpec(memory_space=pl.ANY)
    params = pltpu.CompilerParams(vmem_limit_bytes=VMEM_LIMIT)

    messages = pl.pallas_call(
        pack_kernel,
        out_shape=[shape(6 * slab, LANES)] * count,
        in_specs=[scalar] + [anywhere] * 3,
        out_specs=whole_specs(count),
        scratch_shapes=[pltpu.SemaphoreType.DMA((count, 3))],
        compiler_params=params,
        name="pack",
    )(place, in_hbm(flat_streams), in_hbm(flat_filters), in_hbm(flat_grad))
    arrived = traded(messages, count)
    forward, back = transform_tables(blocks, local_rows * count)
    tables = pl.pallas_call(
        tables_kernel,
        out_shape=[
            shape(3, TAPS, LANES, dtype=F32),
            shape(*forward.shape),
            shape(*back.shape),
        ],
        in_specs=[scalar] + [anywhere] * 4,
        out_specs=whole_specs(3),
        scratch_shapes=[pltpu.SemaphoreType.DMA((3,))],
        compiler_params=params,
        name="tables",
    )(
        place,
        messages[0],
        in_hbm(short_taps),
        in_hbm(jnp.asarray(forward)),
        in_hbm(jnp.asarray(back)),
    )
    answers = core_call(place, arrived, tables, blocks)
    returned = traded(answers, count)

    layer_out, stream_grads, tap_grads = pl.pallas_call(
        functools.partial(home_kernel, blocks, count),
        out_shape=[
            shape(slab, channels),
            shape(3 * slab, channels),
            shape(3, TAPS, channels, dtype=F32),
        ],
        in_specs=[scalar] + whole_specs(count + 3),
        out_specs=whole_specs(3),
        compiler_params=params,
        name="home",
    )(place, *returned, flat_streams[2 * slab :], flat_grad, short_taps)
    return (
        layer_out.reshape(out_grad.shape),
        stream_grads.reshape(streams.shape),
        tap_grads,
    )


def shifted(value, axis, by):
    count = lax.axis_size(axis)
    return lax.ppermute(value, axis, [(i, (i + by) % count) for i in range(count)])


def complex_product(left_real, left_imag, right_real, right_imag):
    return (
        left_real * right_real - left_imag * right_imag,
        left_real * right_imag + left_imag * right_real,
    )


def conj_product(left_real, left_imag, right_real, right_imag):
    return (
        left_real * right_real + left_imag * right_imag,
        left_real * right_imag - left_imag * right_real,
    )


def long_local(streams, short_taps, long_filters, out_grad):
    seq_count = lax.axis_size("seq")
    seq_place = lax.axis_index("seq")
    local_rows = streams.shape[1]
    channels = streams.shape[3]
    block_rows = local_rows * seq_count
    full_length = 2 * block_rows * seq_count
    angle_unit = math.pi / full_length
    block_pos = jnp.arange(seq_count, dtype=jnp.int32)
    odd_slots = 2 * block_pos + 1
    local_index = seq_place * local_rows + jnp.arange(local_rows, dtype=jnp.int32)
    row_pos = jnp.arange(block_rows, dtype=jnp.int32)
    start_pos = block_pos[None, :, None] * block_rows + local_index[:, None, None]
    fwd_angle = (start_pos * odd_slots[None, None, :] % (2 * full_length)).astype(
        jnp.float32
    ) * angle_unit
    fwd_table = jnp.stack([jnp.cos(fwd_angle), -jnp.sin(fwd_angle)], axis=-1)
    inner_angle = (row_pos[:, None] * row_pos[None, :] % block_rows).astype(jnp.float32) * (
        2.0 * math.pi / block_rows
    )
    inner_cos = jnp.cos(inner_angle)
    inner_sin = jnp.sin(inner_angle)
    inner_table = jnp.stack(
        [jnp.stack([inner_cos, -inner_sin], axis=-1), jnp.stack([inner_sin, inner_cos], axis=-1)],
        axis=0,
    )
    back_num = (
        row_pos[None, :]
        * (4 * seq_count * row_pos[:, None] + 2 * seq_place + 1)
        % (2 * full_length)
    )
    back_angle = back_num.astype(jnp.float32) * angle_unit
    back_cos = jnp.cos(back_angle)
    back_sin = jnp.sin(back_angle)
    back_table = jnp.stack(
        [jnp.stack([back_cos, back_sin], axis=-1), jnp.stack([-back_sin, back_cos], axis=-1)],
        axis=0,
    )
    outer_angle = (block_pos[:, None] * odd_slots[None, :] % (4 * seq_count)).astype(
        jnp.float32
    ) * (math.pi / (2 * seq_count))
    outer_table = jnp.stack([jnp.cos(outer_angle).T, -jnp.sin(outer_angle).T], axis=0)

    def previous_rows(block):
        edge = shifted(block[:, -1:], "seq", 1)
        rolled = jnp.concatenate([jnp.zeros_like(edge[:, :, :1]), edge[:, :, :-1]], axis=2)
        edge = jnp.where(seq_place == 0, rolled, edge)
        return jnp.concatenate([edge, block[:, :-1]], axis=1)

    def next_rows(block):
        edge = shifted(block[:, :1], "seq", -1)
        rolled = jnp.concatenate([edge[:, :, 1:], jnp.zeros_like(edge[:, :, :1])], axis=2)
        edge = jnp.where(seq_place == seq_count - 1, rolled, edge)
        return jnp.concatenate([block[:, 1:], edge], axis=1)

    def spectra(signals):
        count = signals.shape[0]
        twisted = jnp.einsum("simc,imjr->srijc", signals, fwd_table, precision=HIGHEST_PRECISION)
        slotted = lax.all_to_all(twisted, "seq", split_axis=3, concat_axis=2, tiled=True)
        slotted = slotted.reshape(count, 2, block_rows, channels)
        spec = jnp.einsum("sric,rikq->sqkc", slotted, inner_table, precision=HIGHEST_PRECISION)
        return (spec[:, 0], spec[:, 1])

    def signals_back(real_spec, imag_spec):
        count = real_spec.shape[0]
        stacked = jnp.stack([real_spec, imag_spec], axis=1)
        turned = jnp.einsum("srkc,rkiq->sqic", stacked, back_table, precision=HIGHEST_PRECISION)
        turned = turned.reshape(count, 2, block_rows, 1, channels)
        parts = lax.all_to_all(turned, "seq", split_axis=2, concat_axis=3, tiled=True)
        rows_out = jnp.einsum("srijc,rjm->simc", parts, outer_table, precision=HIGHEST_PRECISION)
        return rows_out * (2.0 / full_length)

    def tap_weight(index):
        return short_taps[:, index][:, None, None, :]

    prev_one = previous_rows(streams)
    prev_two = previous_rows(prev_one)
    filtered = (
        tap_weight(0) * streams + tap_weight(1) * prev_one + tap_weight(2) * prev_two
    ).astype(jnp.bfloat16)
    value_stream = filtered[0].astype(jnp.float32)
    gate_one = filtered[1].astype(jnp.float32)
    gate_two = filtered[2].astype(jnp.float32)
    filters = long_filters.astype(jnp.float32)
    real_first, imag_first = spectra(jnp.stack([value_stream, filters[0]]))
    product_one = complex_product(real_first[0], imag_first[0], real_first[1], imag_first[1])
    first_conv = signals_back(product_one[0][None], product_one[1][None])[0]
    gated_first = gate_one * first_conv
    real_second, imag_second = spectra(jnp.stack([gated_first, filters[1]]))
    product_two = complex_product(real_second[0], imag_second[0], real_second[1], imag_second[1])
    second_conv = signals_back(product_two[0][None], product_two[1][None])[0]
    layer_out = (gate_two * second_conv).astype(jnp.bfloat16)
    cotangent = out_grad.astype(jnp.float32)
    back_two = cotangent * gate_two
    grad_two = cotangent * second_conv
    real_third, imag_third = spectra(back_two[None])
    filter_two_real, filter_two_imag = (real_second[1], imag_second[1])
    correlated_two = conj_product(filter_two_real, filter_two_imag, real_third[0], imag_third[0])
    grad_gated = signals_back(correlated_two[0][None], correlated_two[1][None])[0]
    grad_one = grad_gated * first_conv
    back_one = grad_gated * gate_one
    real_fourth, imag_fourth = spectra(back_one[None])
    filter_one_real, filter_one_imag = (real_first[1], imag_first[1])
    correlated_one = conj_product(filter_one_real, filter_one_imag, real_fourth[0], imag_fourth[0])
    grad_value = signals_back(correlated_one[0][None], correlated_one[1][None])[0]
    stream_cot = jnp.stack([grad_value, grad_one, grad_two]).astype(jnp.bfloat16)
    next_one = next_rows(stream_cot)
    next_two = next_rows(next_one)
    stream_grads = (
        tap_weight(0) * stream_cot + tap_weight(1) * next_one + tap_weight(2) * next_two
    ).astype(jnp.bfloat16)
    cot_float = stream_cot.astype(jnp.float32)
    tap_terms = jnp.stack(
        [
            jnp.sum(cot_float * streams, axis=(1, 2)),
            jnp.sum(cot_float * prev_one, axis=(1, 2)),
            jnp.sum(cot_float * prev_two, axis=(1, 2)),
        ],
        axis=1,
    )
    tap_total = lax.psum(tap_terms, "seq")
    return (layer_out, stream_grads, tap_total * (1.0 / math.sqrt(block_rows * seq_count)))


def local(streams, short_taps, long_filters, out_grad):
    count = lax.axis_size("seq")
    _, local_rows, blocks, channels = streams.shape
    rows = local_rows * count
    fits = (
        channels == LANES * count
        and count & (count - 1) == 0
        and blocks == 8
        and rows == LANES
        and local_rows >= TAPS - 1
    )
    work = short_local if fits else long_local
    return work(streams, short_taps, long_filters, out_grad)


def solution(mesh):
    in_specs = (
        P(None, "seq", "group", "tensor"),
        P(None, None, "tensor"),
        P(None, "seq", None, "tensor"),
        P("seq", "group", "tensor"),
    )
    out_specs = (
        P("seq", "group", "tensor"),
        P(None, "seq", "group", "tensor"),
        P("group", None, "tensor"),
    )
    return jax.shard_map(local, mesh=mesh, in_specs=in_specs, out_specs=out_specs, check_vma=False)
```

profile of v0, /device:TPU:0, one launch (start us, length us, event | category | flops | bytes accessed | tf_op | source)
XLA Modules:
  0.0 73.2 jit_solution(18431361991485547501)
XLA Ops:
  0.6 1.7 %pack.1 = (bf16[768,128]{1,0:T(8,128)(2,1)S(1)}, bf16[768,128]{1,0:T(8,128)(2,1)S(1)}, bf16[768,128]{1,0:T(8,128)(2,1)S(1)}, bf16[768,128]{1,0:T(8,128)(2,1)S(1)...) custom-call(s32[1]{0:T(128)} %bitcast.me_ref, ...), custom_call_target="tpu_custom_call" | custom-call | tf_op jit(solution)/shard_map/pack/pallas_call | solution.py:415
  2.3 4.0 %collective-permute-start = (bf16[768,128]{1,0:T(8,128)(2,1)S(1)}, bf16[768,128]{1,0:T(8,128)(2,1)S(1)}, u32[]{:S(2)}, u32[]{:S(2)}) collective-permute-start(bf16[768,128]{1,0:T(8,128)(2,1)S(1)} %get-tuple-element.26), channel_id=1, source_target_pairs={{0,6},{2,4},{4,2},{6,0},{8,14},{10,12},{12,10},{14,8},{1,7},{3,5},... | collective-permute-start | bytes 589832 | tf_op jit(solution)/shard_map/ppermute | solution.py:354
  6.3 2.6 %collective-permute-start.1 = (bf16[768,128]{1,0:T(8,128)(2,1)S(1)}, bf16[768,128]{1,0:T(8,128)(2,1)S(1)}, u32[]{:S(2)}, u32[]{:S(2)}) collective-permute-start(bf16[768,128]{1,0:T(8,128)(2,1)S(1)} %get-tuple-element.27), channel_id=1, source_target_pairs={{0,8},{2,10},{4,12},{6,14},{8,0},{10,2},{12,4},{14,6},{1,9},{3,11}... | collective-permute-start | bytes 589832 | tf_op jit(solution)/shard_map/ppermute | solution.py:354
  8.9 0.3 collective-permute-start.2
  9.2 2.5 %collective-permute-start.3 = (bf16[768,128]{1,0:T(8,128)(2,1)S(1)}, bf16[768,128]{1,0:T(8,128)(2,1)S(1)}, u32[]{:S(2)}, u32[]{:S(2)}) collective-permute-start(bf16[768,128]{1,0:T(8,128)(2,1)S(1)} %get-tuple-element.29), channel_id=1, source_target_pairs={{0,12},{2,14},{4,8},{6,10},{8,4},{10,6},{12,0},{14,2},{1,13},{3,15... | collective-permute-start | bytes 589832 | tf_op jit(solution)/shard_map/ppermute | solution.py:354
  11.7 2.3 %collective-permute-start.4 = (bf16[768,128]{1,0:T(8,128)(2,1)S(1)}, bf16[768,128]{1,0:T(8,128)(2,1)S(1)}, u32[]{:S(2)}, u32[]{:S(2)}) collective-permute-start(bf16[768,128]{1,0:T(8,128)(2,1)S(1)} %get-tuple-element.30), channel_id=1, source_target_pairs={{0,14},{2,12},{4,10},{6,8},{8,6},{10,4},{12,2},{14,0},{1,15},{3,13... | collective-permute-start | bytes 589832 | tf_op jit(solution)/shard_map/ppermute | solution.py:354
  14.0 1.3 %collective-permute-done.refs_1_ = bf16[768,128]{1,0:T(8,128)(2,1)S(1)} collective-permute-done((bf16[768,128]{1,0:T(8,128)(2,1)S(1)}, bf16[768,128]{1,0:T(8,128)(2,1)S(1)}, u32[]{:S(2)}, u32[]{:S(2)}) %collective-permute-start) | collective-permute-done | bytes 196640 | tf_op jit(solution)/shard_map/ppermute | solution.py:354
  15.3 0.0 collective-permute-start.5
  15.4 16.6 %collective-permute-done.1.refs_2_ = bf16[768,128]{1,0:T(8,128)(2,1)S(1)} collective-permute-done((bf16[768,128]{1,0:T(8,128)(2,1)S(1)}, bf16[768,128]{1,0:T(8,128)(2,1)S(1)}, u32[]{:S(2)}, u32[]{:S(2)}) %collective-permute-start.1) | collective-permute-done | bytes 196640 | tf_op jit(solution)/shard_map/ppermute | solution.py:354
  31.9 0.3 collective-permute-start.6
  32.3 2.3 %tables.1 = (f32[3,3,128]{2,1,0:T(4,128)S(1)}, bf16[8,512,256]{2,1,0:T(8,128)(2,1)S(1)}, bf16[8,512,256]{2,1,0:T(8,128)(2,1)S(1)}) custom-call(s32[1]{0:T(128)} %bitcast.me_ref, bf16[768,128]{1,0:T(8,128)(2,1)S(1)} %get-tuple-element.25.packed_ref.refs_0_, f32[3,3,1024]{2,1,0:T(4,128)} %refs_10_.1, bf16[8,512,256]{2,1,0:T(8,128)(2,1)} %constant.10.clone.forward_ref, ...), custom_call_target="tpu_custom_call" | custom-call | tf_op jit(solution)/shard_map/tables/pallas_call | solution.py:426
  34.5 1.3 %collective-permute-done.2.refs_3_ = bf16[768,128]{1,0:T(8,128)(2,1)S(1)} collective-permute-done((bf16[768,128]{1,0:T(8,128)(2,1)S(1)}, bf16[768,128]{1,0:T(8,128)(2,1)S(1)}, u32[]{:S(2)}, u32[]{:S(2)}) %collective-permute-start.2) | collective-permute-done | bytes 196640 | tf_op jit(solution)/shard_map/ppermute | solution.py:354
  35.9 0.0 collective-permute-done.3.refs_4_
  35.9 0.0 collective-permute-done.4.refs_5_
  35.9 0.0 collective-permute-done.5.refs_6_
  35.9 1.9 %collective-permute-done.6.refs_7_ = bf16[768,128]{1,0:T(8,128)(2,1)S(1)} collective-permute-done((bf16[768,128]{1,0:T(8,128)(2,1)S(1)}, bf16[768,128]{1,0:T(8,128)(2,1)S(1)}, u32[]{:S(2)}, u32[]{:S(2)}) %collective-permute-start.6) | collective-permute-done | bytes 196640 | tf_op jit(solution)/shard_map/ppermute | solution.py:354
  37.8 0.0 copy-start
  37.8 0.0 copy-start.1
  37.8 10.8 %core.1 = (bf16[432,128]{1,0:T(8,128)(2,1)S(1)}, bf16[432,128]{1,0:T(8,128)(2,1)S(1)}, bf16[432,128]{1,0:T(8,128)(2,1)S(1)}, bf16[432,128]{1,0:T(8,128)(2,1)S(1)...) custom-call(s32[1]{0:T(128)} %bitcast.me_ref, ...), custom_call_target="tpu_custom_call" | custom-call | tf_op jit(solution)/shard_map/core/pallas_call | solution.py:379
  48.6 2.7 %collective-permute-start.10 = (bf16[432,128]{1,0:T(8,128)(2,1)S(1)}, bf16[432,128]{1,0:T(8,128)(2,1)S(1)}, u32[]{:S(2)}, u32[]{:S(2)}) collective-permute-start(bf16[432,128]{1,0:T(8,128)(2,1)S(1)} %get-tuple-element.40), channel_id=1, source_target_pairs={{0,12},{2,14},{4,8},{6,10},{8,4},{10,6},{12,0},{14,2},{1,13},{3,15... | collective-permute-start | bytes 331784 | tf_op jit(solution)/shard_map/ppermute | solution.py:354
  51.4 1.6 %collective-permute-start.11 = (bf16[432,128]{1,0:T(8,128)(2,1)S(1)}, bf16[432,128]{1,0:T(8,128)(2,1)S(1)}, u32[]{:S(2)}, u32[]{:S(2)}) collective-permute-start(bf16[432,128]{1,0:T(8,128)(2,1)S(1)} %get-tuple-element.41), channel_id=1, source_target_pairs={{0,14},{2,12},{4,10},{6,8},{8,6},{10,4},{12,2},{14,0},{1,15},{3,13... | collective-permute-start | bytes 331784 | tf_op jit(solution)/shard_map/ppermute | solution.py:354
  53.0 4.6 %collective-permute-start.12 = (bf16[432,128]{1,0:T(8,128)(2,1)S(1)}, bf16[432,128]{1,0:T(8,128)(2,1)S(1)}, u32[]{:S(2)}, u32[]{:S(2)}) collective-permute-start(bf16[432,128]{1,0:T(8,128)(2,1)S(1)} %get-tuple-element.42), channel_id=1, source_target_pairs={{0,4},{2,6},{4,0},{6,2},{8,12},{10,14},{12,8},{14,10},{1,5},{3,7},... | collective-permute-start | bytes 331784 | tf_op jit(solution)/shard_map/ppermute | solution.py:354
  57.6 0.6 collective-permute-start.13
  58.2 0.9 %collective-permute-start.7 = (bf16[432,128]{1,0:T(8,128)(2,1)S(1)}, bf16[432,128]{1,0:T(8,128)(2,1)S(1)}, u32[]{:S(2)}, u32[]{:S(2)}) collective-permute-start(bf16[432,128]{1,0:T(8,128)(2,1)S(1)} %get-tuple-element.37), channel_id=1, source_target_pairs={{0,6},{2,4},{4,2},{6,0},{8,14},{10,12},{12,10},{14,8},{1,7},{3,5},... | collective-permute-start | bytes 331784 | tf_op jit(solution)/shard_map/ppermute | solution.py:354
  59.1 0.0 collective-permute-done.10.refs_4_
  59.1 3.1 %collective-permute-start.8 = (bf16[432,128]{1,0:T(8,128)(2,1)S(1)}, bf16[432,128]{1,0:T(8,128)(2,1)S(1)}, u32[]{:S(2)}, u32[]{:S(2)}) collective-permute-start(bf16[432,128]{1,0:T(8,128)(2,1)S(1)} %get-tuple-element.38), channel_id=1, source_target_pairs={{0,8},{2,10},{4,12},{6,14},{8,0},{10,2},{12,4},{14,6},{1,9},{3,11}... | collective-permute-start | bytes 331784 | tf_op jit(solution)/shard_map/ppermute | solution.py:354
  62.1 0.0 collective-permute-done.11.refs_5_
  62.1 4.1 %collective-permute-start.9 = (bf16[432,128]{1,0:T(8,128)(2,1)S(1)}, bf16[432,128]{1,0:T(8,128)(2,1)S(1)}, u32[]{:S(2)}, u32[]{:S(2)}) collective-permute-start(bf16[432,128]{1,0:T(8,128)(2,1)S(1)} %get-tuple-element.39), channel_id=1, source_target_pairs={{0,10},{2,8},{4,14},{6,12},{8,2},{10,0},{12,6},{14,4},{1,11},{3,9}... | collective-permute-start | bytes 331784 | tf_op jit(solution)/shard_map/ppermute | solution.py:354
  66.3 1.0 %slice_bitcast_fusion.refs_8_ = bf16[128,1024]{1,0:T(8,128)(2,1)S(1)} fusion(bf16[3,16,8,1024]{3,2,1,0:T(8,128)(2,1)} %param.6), kind=kLoop, calls=%fused_computation | loop fusion | bytes 524288 | tf_op jit(solution)/shard_map/slice | solution.py:459
  67.3 0.0 collective-permute-done.12.refs_6_
  67.3 0.0 collective-permute-done.13.refs_7_
  67.3 0.0 collective-permute-done.7.refs_1_
  67.3 1.7 %collective-permute-done.8.refs_2_ = bf16[432,128]{1,0:T(8,128)(2,1)S(1)} collective-permute-done((bf16[432,128]{1,0:T(8,128)(2,1)S(1)}, bf16[432,128]{1,0:T(8,128)(2,1)S(1)}, u32[]{:S(2)}, u32[]{:S(2)}) %collective-permute-start.8) | collective-permute-done | bytes 110624 | tf_op jit(solution)/shard_map/ppermute | solution.py:354
  69.0 2.8 %collective-permute-done.9.refs_3_ = bf16[432,128]{1,0:T(8,128)(2,1)S(1)} collective-permute-done((bf16[432,128]{1,0:T(8,128)(2,1)S(1)}, bf16[432,128]{1,0:T(8,128)(2,1)S(1)}, u32[]{:S(2)}, u32[]{:S(2)}) %collective-permute-start.9) | collective-permute-done | bytes 110624 | tf_op jit(solution)/shard_map/ppermute | solution.py:354
  71.8 0.0 copy-done
  71.8 0.0 copy-done.1
  71.8 1.4 %home.1 = (bf16[128,1024]{1,0:T(8,128)(2,1)}, bf16[384,1024]{1,0:T(8,128)(2,1)}, f32[3,3,1024]{2,1,0:T(4,128)}) custom-call(s32[1]{0:T(128)} %bitcast.me_ref, bf16[432,128]{1,0:T(8,128)(2,1)S(1)} %get-tuple-element.36.refs_0_, bf16[432,128]{1,0:T(8,128)(2,1)S(1)} %collective-permute-done.7.refs_1_, bf16[432,128]{1,0:T(8,128)(2,1)S(1)} %collective-permute-done.8.refs_2_, ...), custom_call_target="tpu_custom_call" | custom-call | tf_op jit(solution)/shard_map/home/pallas_call | solution.py:448
Async XLA Ops:
  2.3 13.0 %collective-permute-start = (bf16[768,128]{1,0:T(8,128)(2,1)S(1)}, bf16[768,128]{1,0:T(8,128)(2,1)S(1)}, u32[]{:S(2)}, u32[]{:S(2)}) collective-permute-start(bf16[768,128]{1,0:T(8,128)(2,1)S(1)} %get-tuple-element.26), channel_id=1, source_target_pairs={{0,6},{2,4},{4,2},{6,0},{8,14},{10,12},{12,10},{14,8},{1,7},{3,5},... | collective-permute-start | bytes 589832 | tf_op jit(solution)/shard_map/ppermute | solution.py:354
  6.3 25.6 %collective-permute-start.1 = (bf16[768,128]{1,0:T(8,128)(2,1)S(1)}, bf16[768,128]{1,0:T(8,128)(2,1)S(1)}, u32[]{:S(2)}, u32[]{:S(2)}) collective-permute-start(bf16[768,128]{1,0:T(8,128)(2,1)S(1)} %get-tuple-element.27), channel_id=1, source_target_pairs={{0,8},{2,10},{4,12},{6,14},{8,0},{10,2},{12,4},{14,6},{1,9},{3,11}... | collective-permute-start | bytes 589832 | tf_op jit(solution)/shard_map/ppermute | solution.py:354
  8.9 26.9 %collective-permute-start.2 = (bf16[768,128]{1,0:T(8,128)(2,1)S(1)}, bf16[768,128]{1,0:T(8,128)(2,1)S(1)}, u32[]{:S(2)}, u32[]{:S(2)}) collective-permute-start(bf16[768,128]{1,0:T(8,128)(2,1)S(1)} %get-tuple-element.28), channel_id=1, source_target_pairs={{0,10},{2,8},{4,14},{6,12},{8,2},{10,0},{12,6},{14,4},{1,11},{3,9}... | collective-permute-start | bytes 589832 | tf_op jit(solution)/shard_map/ppermute | solution.py:354
  9.2 26.6 %collective-permute-start.3 = (bf16[768,128]{1,0:T(8,128)(2,1)S(1)}, bf16[768,128]{1,0:T(8,128)(2,1)S(1)}, u32[]{:S(2)}, u32[]{:S(2)}) collective-permute-start(bf16[768,128]{1,0:T(8,128)(2,1)S(1)} %get-tuple-element.29), channel_id=1, source_target_pairs={{0,12},{2,14},{4,8},{6,10},{8,4},{10,6},{12,0},{14,2},{1,13},{3,15... | collective-permute-start | bytes 589832 | tf_op jit(solution)/shard_map/ppermute | solution.py:354
  11.7 24.1 %collective-permute-start.4 = (bf16[768,128]{1,0:T(8,128)(2,1)S(1)}, bf16[768,128]{1,0:T(8,128)(2,1)S(1)}, u32[]{:S(2)}, u32[]{:S(2)}) collective-permute-start(bf16[768,128]{1,0:T(8,128)(2,1)S(1)} %get-tuple-element.30), channel_id=1, source_target_pairs={{0,14},{2,12},{4,10},{6,8},{8,6},{10,4},{12,2},{14,0},{1,15},{3,13... | collective-permute-start | bytes 589832 | tf_op jit(solution)/shard_map/ppermute | solution.py:354
  15.3 20.5 %collective-permute-start.5 = (bf16[768,128]{1,0:T(8,128)(2,1)S(1)}, bf16[768,128]{1,0:T(8,128)(2,1)S(1)}, u32[]{:S(2)}, u32[]{:S(2)}) collective-permute-start(bf16[768,128]{1,0:T(8,128)(2,1)S(1)} %get-tuple-element.31), channel_id=1, source_target_pairs={{0,4},{2,6},{4,0},{6,2},{8,12},{10,14},{12,8},{14,10},{1,5},{3,7},... | collective-permute-start | bytes 589832 | tf_op jit(solution)/shard_map/ppermute | solution.py:354
  31.9 5.9 %collective-permute-start.6 = (bf16[768,128]{1,0:T(8,128)(2,1)S(1)}, bf16[768,128]{1,0:T(8,128)(2,1)S(1)}, u32[]{:S(2)}, u32[]{:S(2)}) collective-permute-start(bf16[768,128]{1,0:T(8,128)(2,1)S(1)} %get-tuple-element.32), channel_id=1, source_target_pairs={{0,2},{2,0},{4,6},{6,4},{8,10},{10,8},{12,14},{14,12},{1,3},{3,1},... | collective-permute-start | bytes 589832 | tf_op jit(solution)/shard_map/ppermute | solution.py:354
  37.8 34.0 %copy-start = (bf16[16,8,1024]{2,1,0:T(8,128)(2,1)S(1)}, bf16[16,8,1024]{2,1,0:T(8,128)(2,1)}, u32[]{:S(2)}) copy-start(bf16[16,8,1024]{2,1,0:T(8,128)(2,1)} %param.9) | copy-start | bytes 786436
  37.8 34.0 %copy-start.1 = (f32[3,3,1024]{2,1,0:T(4,128)S(1)}, f32[3,3,1024]{2,1,0:T(4,128)}, u32[]{:S(2)}) copy-start(f32[3,3,1024]{2,1,0:T(4,128)} %refs_10_.1) | copy-start | bytes 110596
  48.6 10.4 %collective-permute-start.10 = (bf16[432,128]{1,0:T(8,128)(2,1)S(1)}, bf16[432,128]{1,0:T(8,128)(2,1)S(1)}, u32[]{:S(2)}, u32[]{:S(2)}) collective-permute-start(bf16[432,128]{1,0:T(8,128)(2,1)S(1)} %get-tuple-element.40), channel_id=1, source_target_pairs={{0,12},{2,14},{4,8},{6,10},{8,4},{10,6},{12,0},{14,2},{1,13},{3,15... | collective-permute-start | bytes 331784 | tf_op jit(solution)/shard_map/ppermute | solution.py:354
  51.4 10.8 %collective-permute-start.11 = (bf16[432,128]{1,0:T(8,128)(2,1)S(1)}, bf16[432,128]{1,0:T(8,128)(2,1)S(1)}, u32[]{:S(2)}, u32[]{:S(2)}) collective-permute-start(bf16[432,128]{1,0:T(8,128)(2,1)S(1)} %get-tuple-element.41), channel_id=1, source_target_pairs={{0,14},{2,12},{4,10},{6,8},{8,6},{10,4},{12,2},{14,0},{1,15},{3,13... | collective-permute-start | bytes 331784 | tf_op jit(solution)/shard_map/ppermute | solution.py:354
  53.0 14.3 %collective-permute-start.12 = (bf16[432,128]{1,0:T(8,128)(2,1)S(1)}, bf16[432,128]{1,0:T(8,128)(2,1)S(1)}, u32[]{:S(2)}, u32[]{:S(2)}) collective-permute-start(bf16[432,128]{1,0:T(8,128)(2,1)S(1)} %get-tuple-element.42), channel_id=1, source_target_pairs={{0,4},{2,6},{4,0},{6,2},{8,12},{10,14},{12,8},{14,10},{1,5},{3,7},... | collective-permute-start | bytes 331784 | tf_op jit(solution)/shard_map/ppermute | solution.py:354
  57.6 9.7 %collective-permute-start.13 = (bf16[432,128]{1,0:T(8,128)(2,1)S(1)}, bf16[432,128]{1,0:T(8,128)(2,1)S(1)}, u32[]{:S(2)}, u32[]{:S(2)}) collective-permute-start(bf16[432,128]{1,0:T(8,128)(2,1)S(1)} %get-tuple-element.43), channel_id=1, source_target_pairs={{0,2},{2,0},{4,6},{6,4},{8,10},{10,8},{12,14},{14,12},{1,3},{3,1},... | collective-permute-start | bytes 331784 | tf_op jit(solution)/shard_map/ppermute | solution.py:354
  58.2 9.1 %collective-permute-start.7 = (bf16[432,128]{1,0:T(8,128)(2,1)S(1)}, bf16[432,128]{1,0:T(8,128)(2,1)S(1)}, u32[]{:S(2)}, u32[]{:S(2)}) collective-permute-start(bf16[432,128]{1,0:T(8,128)(2,1)S(1)} %get-tuple-element.37), channel_id=1, source_target_pairs={{0,6},{2,4},{4,2},{6,0},{8,14},{10,12},{12,10},{14,8},{1,7},{3,5},... | collective-permute-start | bytes 331784 | tf_op jit(solution)/shard_map/ppermute | solution.py:354
  59.1 10.0 %collective-permute-start.8 = (bf16[432,128]{1,0:T(8,128)(2,1)S(1)}, bf16[432,128]{1,0:T(8,128)(2,1)S(1)}, u32[]{:S(2)}, u32[]{:S(2)}) collective-permute-start(bf16[432,128]{1,0:T(8,128)(2,1)S(1)} %get-tuple-element.38), channel_id=1, source_target_pairs={{0,8},{2,10},{4,12},{6,14},{8,0},{10,2},{12,4},{14,6},{1,9},{3,11}... | collective-permute-start | bytes 331784 | tf_op jit(solution)/shard_map/ppermute | solution.py:354
  62.1 9.7 %collective-permute-start.9 = (bf16[432,128]{1,0:T(8,128)(2,1)S(1)}, bf16[432,128]{1,0:T(8,128)(2,1)S(1)}, u32[]{:S(2)}, u32[]{:S(2)}) collective-permute-start(bf16[432,128]{1,0:T(8,128)(2,1)S(1)} %get-tuple-element.39), channel_id=1, source_target_pairs={{0,10},{2,8},{4,14},{6,12},{8,2},{10,0},{12,6},{14,4},{1,11},{3,9}... | collective-permute-start | bytes 331784 | tf_op jit(solution)/shard_map/ppermute | solution.py:354
where the time goes:
time: 73.4 us; the launch traced here: 73.2 us
  starting transfers between devices  29.6 us (40%)
  waiting for transfers between devices  25.7 us (35%)
  Pallas kernels  16.2 us (22%)
  local copies, waits for them, and re-layouts  0.97 us (1%)
    ppermute x14, starting transfers between devices, traded(): out.append(lax.ppermute(message, 'seq', [(i, i ^ k) for i in range(count)]))  29.6 us
    ppermute x14, waiting for transfers between devices, traded(): out.append(lax.ppermute(message, 'seq', [(i, i ^ k) for i in range(count)]))  25.7 us
    pallas_call x1, Pallas kernels, core_call(): pl.pallas_call(functools.partial(core_kernel, blocks, count), out_shape=[...  10.8 us
    pallas_call x1, Pallas kernels, short_local(): pl.pallas_call(tables_kernel, out_shape=[shape(3, TAPS, LANES, dtype=F32)...  2.26 us
    pallas_call x1, Pallas kernels, short_local(): pl.pallas_call(pack_kernel, out_shape=[shape(6 * slab, LANES)] * count, i...  1.69 us
  transfers between devices with their start and end apart: 14, of which 6 were waited for; matrix products, arithmetic and copies ran while one was open for 1% of the time, Pallas kernels for 3%

commit v1 on v0

--- a/solution.py
+++ b/solution.py
@@ -99,26 +99,29 @@
     return jnp.where(block == empty, 0.0, rolled)
 
 
-def pack_kernel(me_ref, streams_ref, filters_ref, grad_ref, *refs):
-    outs, sems = refs[:-1], refs[-1]
-    slab = grad_ref.shape[0]
-    me = me_ref[0]
-    copies = []
-    for k, (by, out) in enumerate(zip(sending_order(len(outs)), outs)):
-        lanes = pl.ds(pl.multiple_of((me ^ by) * LANES, LANES), LANES)
-        at = 0
-        for part, source in enumerate((streams_ref, filters_ref, grad_ref)):
-            size = source.shape[0]
-            copies.append(
-                pltpu.make_async_copy(
-                    source.at[:, lanes], out.at[pl.ds(at, size)], sems.at[k, part]
-                )
-            )
-            at += size
+def run_copies(pairs, sems):
+    copies = [
+        pltpu.make_async_copy(source, target, sems.at[n])
+        for n, (source, target) in enumerate(pairs)
+    ]
     for copy in copies:
         copy.start()
     for copy in copies:
         copy.wait()
+
+
+def pack_kernel(me_ref, streams_ref, filters_ref, grad_ref, *refs):
+    outs, sems = refs[:-1], refs[-1]
+    me = me_ref[0]
+    pairs = []
+    for by, out in zip(sending_order(len(outs)), outs):
+        lanes = pl.ds(pl.multiple_of((me ^ by) * LANES, LANES), LANES)
+        at = 0
+        for source in (streams_ref, filters_ref, grad_ref):
+            size = source.shape[0]
+            pairs.append((source.at[:, lanes], out.at[pl.ds(at, size)]))
+            at += size
+    run_copies(pairs, sems)
 
 
 def tables_kernel(me_ref, packed_ref, taps_ref, forward_ref, back_ref, *refs):
@@ -126,146 +129,164 @@
     outs, sems = refs[:-1], refs[-1]
     lanes = pl.ds(pl.multiple_of(me_ref[0] * LANES, LANES), LANES)
     sources = (taps_ref.at[:, :, lanes], forward_ref, back_ref)
-    copies = [
-        pltpu.make_async_copy(source, out, sems.at[n])
-        for n, (source, out) in enumerate(zip(sources, outs))
-    ]
-    for copy in copies:
-        copy.start()
-    for copy in copies:
-        copy.wait()
-
-
-def core_kernel(blocks, partners, me_ref, *refs):
-    msgs = refs[:partners]
-    weights, fwd_ref, back_ref = refs[partners : partners + 3]
-    outs = refs[partners + 3 : 2 * partners + 3]
-    scratch = refs[2 * partners + 3 :]
-    raw, sig, gate, grad, zh, zl, spec, turned, cot, conv, grads = scratch
+    run_copies(zip(sources, outs), sems)
+
+
+class Transforms:
+    def __init__(self, rows, fwd_ref, back_ref, high, low):
+        self.rows, self.fwd, self.back, self.high, self.low = rows, fwd_ref, back_ref, high, low
+        self.blocks = fwd_ref.shape[0]
+
+    def store(self, parts, row, col):
+        for j, (real, imag) in enumerate(odd_transform(parts)):
+            for at, value in ((row, real), (self.rows + row, imag)):
+                high, low = split_bf16(value)
+                self.high[j, pl.ds(at, CHUNK), col : col + LANES] = high
+                self.low[j, pl.ds(at, CHUNK), col : col + LANES] = low
+
+    def times(self, table, j, high, low):
+        size = 2 * self.rows
+        main = jnp.dot(table[j, 0:size], high, preferred_element_type=F32)
+        main += jnp.dot(table[j, 0:size], low, preferred_element_type=F32)
+        return main + jnp.dot(table[j, size : 2 * size], high, preferred_element_type=F32)
+
+    def forward(self, j, begin, end):
+        return self.times(self.fwd, j, self.high[j, :, begin:end], self.low[j, :, begin:end])
+
+    def backward(self, j, data):
+        return self.times(self.back, j, *split_bf16(data))
+
+    def blocks_of(self, slots, row, col):
+        return odd_transform_back(
+            [
+                (
+                    slots[j, pl.ds(row, CHUNK), col : col + LANES],
+                    slots[j, pl.ds(self.rows + row, CHUNK), col : col + LANES],
+                )
+                for j in range(self.blocks)
+            ]
+        )
+
+    def each_slot(self, body):
+        for j in range(self.blocks):
+            body(j)
+
+    def each_chunk(self, body):
+        @pl.loop(0, self.rows // CHUNK, unroll=8)
+        def _(step):
+            body(pl.multiple_of(step * CHUNK, CHUNK))
+
+
+def spread(blocks, row, block):
+    return pl.ds(row * blocks + block, CHUNK, stride=blocks)
+
+
+def product(left, right, conjugate=False):
+    rows = left.shape[0] // 2
+    a_real, a_imag, b_real, b_imag = left[:rows], left[rows:], right[:rows], right[rows:]
+    if conjugate:
+        real, imag = a_real * b_real + a_imag * b_imag, a_imag * b_real - a_real * b_imag
+    else:
+        real, imag = a_real * b_real - a_imag * b_imag, a_real * b_imag + a_imag * b_real
+    return jnp.concatenate([real, imag], axis=0)
+
+
+def filtered(raw, weights, s, at, blocks, size):
+    now = weights[s, 0:1] * raw[pl.ds(at + 2 * blocks, size)]
+    now = now + weights[s, 1:2] * raw[pl.ds(at + blocks, size)]
+    return (now + weights[s, 2:3] * raw[pl.ds(at, size)]).astype(BF16).astype(F32)
+
+
+def core_kernel(blocks, count, me_ref, *refs):
+    weights, fwd_ref, back_ref = refs[:3]
+    msgs, outs, scratch = refs[3 : 3 + count], refs[3 + count : 3 + 2 * count], refs[3 + 2 * count :]
+    raw, sig, gate, grad, high, low, spec, turned, cot, conv, grads = scratch
     me = me_ref[0]
     total = sig.shape[1]
     rows = total // blocks
-    slab = total // partners
+    slab = total // count
     halo = (TAPS - 1) * blocks
 
     def weight(stream, tap):
         return weights[stream, tap : tap + 1]
 
-    for k, by in enumerate(sending_order(partners)):
+    for by, msg in zip(sending_order(count), msgs):
         start = pl.multiple_of((me ^ by) * slab, slab)
         for s in range(3):
-            raw[s, pl.ds(halo + start, slab)] = msgs[k][s * slab : (s + 1) * slab].astype(F32)
-        sig[2, pl.ds(start, slab)] = msgs[k][3 * slab : 4 * slab].astype(F32)
-        sig[3, pl.ds(start, slab)] = msgs[k][4 * slab : 5 * slab].astype(F32)
-        grad[pl.ds(start, slab)] = msgs[k][5 * slab : 6 * slab].astype(F32)
+            raw[s, pl.ds(halo + start, slab)] = msg[s * slab : (s + 1) * slab].astype(F32)
+        for f in range(2):
+            sig[f, pl.ds(start, slab)] = msg[(3 + f) * slab : (4 + f) * slab].astype(F32)
+        grad[pl.ds(start, slab)] = msg[5 * slab : 6 * slab].astype(F32)
     for s in range(3):
         raw[s, 0:halo] = shift_blocks(raw[s, total : total + halo], blocks, 1)
 
     @pl.loop(0, total // slab)
     def _(step):
         base = pl.multiple_of(step * slab, slab)
-
-        def filtered(s):
-            now = raw[s, pl.ds(base + 2 * blocks, slab)]
-            prev_one = raw[s, pl.ds(base + blocks, slab)]
-            prev_two = raw[s, pl.ds(base, slab)]
-            both = weight(s, 0) * now + weight(s, 1) * prev_one + weight(s, 2) * prev_two
-            return both.astype(BF16).astype(F32)
-
-        sig[0, pl.ds(base, slab)] = filtered(0)
-        gate[pl.ds(base, slab)] = filtered(1)
-        sig[1, pl.ds(base, slab)] = filtered(2) * grad[pl.ds(base, slab)]
-
-    def store_slots(parts, row, col):
-        for j, (real, imag) in enumerate(odd_transform(parts)):
-            for at, value in ((row, real), (rows + row, imag)):
-                high, low = split_bf16(value)
-                zh[j, pl.ds(at, CHUNK), col : col + LANES] = high
-                zl[j, pl.ds(at, CHUNK), col : col + LANES] = low
-
-    def times(table, j, high, low):
-        size = 2 * rows
-        main = jnp.dot(table[j, 0:size], high, preferred_element_type=F32)
-        main += jnp.dot(table[j, 0:size], low, preferred_element_type=F32)
-        return main + jnp.dot(table[j, size : 2 * size], high, preferred_element_type=F32)
-
-    @pl.loop(0, rows // CHUNK)
-    def _(step):
-        row = pl.multiple_of(step * CHUNK, CHUNK)
-        for s in range(4):
-            parts = [
-                sig[s, pl.ds(row * blocks + b, CHUNK, stride=blocks)] for b in range(blocks)
-            ]
-            store_slots(parts, row, s * LANES)
-
-    def products(data, first, second):
-        real, imag = data[:rows], data[rows:]
-        a_real, a_imag = real[:, :LANES], imag[:, :LANES]
-        c_real, c_imag = real[:, LANES:], imag[:, LANES:]
-        (f_real, f_imag), (s_real, s_imag) = first, second
-        left = jnp.concatenate(
-            [a_real * f_real - a_imag * f_imag, a_real * f_imag + a_imag * f_real], axis=0
-        )
-        right = jnp.concatenate(
-            [c_real * s_real + c_imag * s_imag, c_imag * s_real - c_real * s_imag], axis=0
-        )
-        return jnp.concatenate([left, right], axis=1)
-
-    def filter_spec(j, f):
-        cols = slice(f * LANES, (f + 1) * LANES)
-        return spec[j, 0:rows, cols], spec[j, rows : 2 * rows, cols]
-
-    @pl.loop(0, blocks, unroll=blocks)
-    def _(j):
-        data = times(fwd_ref, j, zh[j], zl[j])
-        spec[j] = data[:, 2 * LANES :]
-        high, low = split_bf16(
-            products(data[:, : 2 * LANES], filter_spec(j, 0), filter_spec(j, 1))
-        )
-        turned[j] = times(back_ref, j, high, low)
-
-    def blocks_of(row, col):
-        return odd_transform_back(
-            [
-                (
-                    turned[j, pl.ds(row, CHUNK), col : col + LANES],
-                    turned[j, pl.ds(rows + row, CHUNK), col : col + LANES],
-                )
-                for j in range(blocks)
-            ]
-        )
-
-    @pl.loop(0, rows // CHUNK)
-    def _(step):
-        row = pl.multiple_of(step * CHUNK, CHUNK)
-        first = blocks_of(row, 0)
-        gated_grad = blocks_of(row, LANES)
+        sig[2, pl.ds(base, slab)] = filtered(raw.at[0], weights, 0, base, blocks, slab)
+        gate[pl.ds(base, slab)] = filtered(raw.at[1], weights, 1, base, blocks, slab)
+        gate_two = filtered(raw.at[2], weights, 2, base, blocks, slab)
+        sig[3, pl.ds(base, slab)] = gate_two * grad[pl.ds(base, slab)]
+
+    work = Transforms(rows, fwd_ref, back_ref, high, low)
+
+    def butterflies(row, signals):
+        for s in signals:
+            parts = [sig[s, spread(blocks, row, b)] for b in range(blocks)]
+            work.store(parts, row, s * LANES)
+
+    work.each_chunk(functools.partial(butterflies, signals=(0, 1)))
+    steps = rows // CHUNK
+    for j in range(max(blocks, steps)):
+        if j < blocks:
+            spec[j] = work.forward(j, 0, 2 * LANES)
+        if j < steps:
+            butterflies(j * CHUNK, (2, 3))
+
+    def forward_data(j):
+        turned[j] = work.forward(j, 2 * LANES, 4 * LANES)
+
+    def first_products(j):
+        data = turned[j]
+        left = product(data[:, :LANES], spec[j, :, :LANES])
+        right = product(data[:, LANES:], spec[j, :, LANES:], True)
+        turned[j] = work.backward(j, jnp.concatenate([left, right], axis=1))
+
+    work.each_slot(forward_data)
+    work.each_slot(first_products)
+
+    def gates(row):
+        first = work.blocks_of(turned, row, 0)
+        gated_grad = work.blocks_of(turned, row, LANES)
         forward, backward = [], []
         for b in range(blocks):
-            place = pl.ds(row * blocks + b, CHUNK, stride=blocks)
-            gate_one = gate[place]
-            cot[1, place] = (gated_grad[b] * first[b]).astype(BF16).astype(F32)
+            here = spread(blocks, row, b)
+            gate_one = gate[here]
+            cot[1, here] = (gated_grad[b] * first[b]).astype(BF16).astype(F32)
             forward.append(gate_one * first[b])
             backward.append(gate_one * gated_grad[b])
-        store_slots(forward, row, 0)
-        store_slots(backward, row, LANES)
-
-    @pl.loop(0, blocks, unroll=blocks)
-    def _(j):
-        data = times(fwd_ref, j, zh[j, :, : 2 * LANES], zl[j, :, : 2 * LANES])
-        high, low = split_bf16(products(data, filter_spec(j, 1), filter_spec(j, 0)))
-        turned[j] = times(back_ref, j, high, low)
-
-    @pl.loop(0, rows // CHUNK)
-    def _(step):
-        row = pl.multiple_of(step * CHUNK, CHUNK)
-        second = blocks_of(row, 0)
-        value_grad = blocks_of(row, LANES)
+        work.store(forward, row, 0)
+        work.store(backward, row, LANES)
+
+    work.each_chunk(gates)
+
+    def convolve(j):
+        data = work.forward(j, 0, 2 * LANES)
+        left = product(data[:, :LANES], spec[j, :, LANES:])
+        right = product(data[:, LANES:], spec[j, :, :LANES], True)
+        turned[j] = work.backward(j, jnp.concatenate([left, right], axis=1))
+
+    work.each_slot(convolve)
+
+    def last(row):
+        second = work.blocks_of(turned, row, 0)
+        value_grad = work.blocks_of(turned, row, LANES)
         for b in range(blocks):
-            place = pl.ds(row * blocks + b, CHUNK, stride=blocks)
-            conv[place] = second[b]
-            cot[0, place] = value_grad[b].astype(BF16).astype(F32)
-
+            here = spread(blocks, row, b)
+            conv[here] = second[b]
+            cot[0, here] = value_grad[b].astype(BF16).astype(F32)
+
+    work.each_chunk(last)
     for s in range(2):
         cot[s, total : total + halo] = shift_blocks(cot[s, 0:halo], blocks, -1)
 
@@ -295,7 +316,7 @@
     tap_rows = [jnp.sum(part, axis=0, keepdims=True) * scale for part in sums]
     pad = jnp.zeros((TAP_ROWS - 3 * TAPS, LANES), F32)
     tap_block = jnp.concatenate(tap_rows + [pad], axis=0).astype(BF16)
-    for k, by in enumerate(sending_order(partners)):
+    for k, by in enumerate(sending_order(count)):
         start = pl.multiple_of((me ^ by) * slab, slab)
         outs[k][0:slab] = conv[pl.ds(start, slab)].astype(BF16)
         for s in range(2):
@@ -348,10 +369,11 @@
     return [0] + far + [k for k in (2, 1) if k < count]
 
 
-def traded(messages, count):
+def everyone(messages):
+    count = len(messages)
     out = [messages[0]]
-    for k, message in zip(sending_order(count)[1:], messages[1:]):
-        out.append(lax.ppermute(message, "seq", [(i, i ^ k) for i in range(count)]))
+    for by, message in zip(sending_order(count)[1:], messages[1:]):
+        out.append(lax.ppermute(message, "seq", [(i, i ^ by) for i in range(count)]))
     return out
 
 
@@ -367,42 +389,48 @@
     return jax.ShapeDtypeStruct(dims, dtype)
 
 
-def core_call(place, arrived, tables, blocks):
-    count = len(arrived)
-    slab = arrived[0].shape[0] // 6
+def call(kernel, name, out_shape, in_specs, scratch=()):
+    return pl.pallas_call(
+        kernel,
+        out_shape=out_shape,
+        in_specs=in_specs,
+        out_specs=whole_specs(len(out_shape)),
+        scratch_shapes=list(scratch),
+        compiler_params=pltpu.CompilerParams(vmem_limit_bytes=VMEM_LIMIT),
+        name=name,
+    )
+
+
+def core_call(place, tables, messages, blocks):
+    count = len(messages)
+    slab = messages[0].shape[0] // 6
     total = slab * count
-    rows = total // blocks
+    spectrum = (blocks, 2 * total // blocks)
     halo = (TAPS - 1) * blocks
-    scalar = pl.BlockSpec(memory_space=pltpu.SMEM)
-    params = pltpu.CompilerParams(vmem_limit_bytes=VMEM_LIMIT)
-    answer_rows = 3 * slab + 2 * halo + TAP_ROWS
-    return pl.pallas_call(
+    return call(
         functools.partial(core_kernel, blocks, count),
-        out_shape=[shape(answer_rows, LANES)] * count,
-        in_specs=[scalar] + whole_specs(count + 3),
-        out_specs=whole_specs(count),
-        scratch_shapes=[
+        "core",
+        [shape(3 * slab + 2 * halo + TAP_ROWS, LANES)] * count,
+        [pl.BlockSpec(memory_space=pltpu.SMEM)] + whole_specs(count + 3),
+        [
             pltpu.VMEM((3, halo + total, LANES), F32),
             pltpu.VMEM((4, total, LANES), F32),
             pltpu.VMEM((total, LANES), F32),
             pltpu.VMEM((total, LANES), F32),
-            pltpu.VMEM((blocks, 2 * rows, 4 * LANES), BF16),
-            pltpu.VMEM((blocks, 2 * rows, 4 * LANES), BF16),
-            pltpu.VMEM((blocks, 2 * rows, 2 * LANES), F32),
-            pltpu.VMEM((blocks, 2 * rows, 2 * LANES), F32),
+            pltpu.VMEM((*spectrum, 4 * LANES), BF16),
+            pltpu.VMEM((*spectrum, 4 * LANES), BF16),
+            pltpu.VMEM((*spectrum, 2 * LANES), F32),
+            pltpu.VMEM((*spectrum, 2 * LANES), F32),
             pltpu.VMEM((3, total + halo, LANES), F32),
             pltpu.VMEM((total, LANES), F32),
             pltpu.VMEM((2, total, LANES), BF16),
         ],
-        compiler_params=params,
-        name="core",
-    )(place, *arrived, *tables)
+    )(place, *tables, *messages)
 
 
 def short_local(streams, short_taps, long_filters, out_grad):
     count = lax.axis_size("seq")
-    me = lax.axis_index("seq").astype(jnp.int32)
-    place = me[None]
+    place = lax.axis_index("seq").astype(jnp.int32)[None]
     _, local_rows, blocks, channels = streams.shape
     slab = local_rows * blocks
     flat_streams = streams.reshape(3 * slab, channels)
@@ -410,52 +438,40 @@
     flat_grad = out_grad.reshape(slab, channels)
     scalar = pl.BlockSpec(memory_space=pltpu.SMEM)
     anywhere = pl.BlockSpec(memory_space=pl.ANY)
-    params = pltpu.CompilerParams(vmem_limit_bytes=VMEM_LIMIT)
-
-    messages = pl.pallas_call(
+
+    packed = call(
         pack_kernel,
-        out_shape=[shape(6 * slab, LANES)] * count,
-        in_specs=[scalar] + [anywhere] * 3,
-        out_specs=whole_specs(count),
-        scratch_shapes=[pltpu.SemaphoreType.DMA((count, 3))],
-        compiler_params=params,
-        name="pack",
+        "pack",
+        [shape(6 * slab, LANES)] * count,
+        [scalar] + [anywhere] * 3,
+        [pltpu.SemaphoreType.DMA((3 * count,))],
     )(place, in_hbm(flat_streams), in_hbm(flat_filters), in_hbm(flat_grad))
-    arrived = traded(messages, count)
+    messages = everyone(packed)
     forward, back = transform_tables(blocks, local_rows * count)
-    tables = pl.pallas_call(
+    tables = call(
         tables_kernel,
-        out_shape=[
-            shape(3, TAPS, LANES, dtype=F32),
-            shape(*forward.shape),
-            shape(*back.shape),
-        ],
-        in_specs=[scalar] + [anywhere] * 4,
-        out_specs=whole_specs(3),
-        scratch_shapes=[pltpu.SemaphoreType.DMA((3,))],
-        compiler_params=params,
-        name="tables",
+        "tables",
+        [shape(3, TAPS, LANES, dtype=F32), shape(*forward.shape), shape(*back.shape)],
+        [scalar] + [anywhere] * 4,
+        [pltpu.SemaphoreType.DMA((3,))],
     )(
         place,
-        messages[0],
+        packed[0],
         in_hbm(short_taps),
         in_hbm(jnp.asarray(forward)),
         in_hbm(jnp.asarray(back)),
     )
-    answers = core_call(place, arrived, tables, blocks)
-    returned = traded(answers, count)
-
-    layer_out, stream_grads, tap_grads = pl.pallas_call(
+    answers = core_call(place, tables, messages, blocks)
+    returned = everyone(answers)
+    layer_out, stream_grads, tap_grads = call(
         functools.partial(home_kernel, blocks, count),
-        out_shape=[
+        "home",
+        [
             shape(slab, channels),
             shape(3 * slab, channels),
             shape(3, TAPS, channels, dtype=F32),
         ],
-        in_specs=[scalar] + whole_specs(count + 3),
-        out_specs=whole_specs(3),
-        compiler_params=params,
-        name="home",
+        [scalar] + whole_specs(count + 3),
     )(place, *returned, flat_streams[2 * slab :], flat_grad, short_taps)
     return (
         layer_out.reshape(out_grad.shape),

time: 73.4 us -> 72.2 us (0.984)
  Pallas kernels: 16.2 us -> 15 us
    pallas_call x4, Pallas kernels: 16.2 us -> 15 us  [the longest x1 9.59 us: core_call(): call(functools.partial(core_kernel, blocks, count), 'core', [shape(3 * sl...]
where the time goes in v1:
time: 72.2 us; the launch traced here: 72 us
  starting transfers between devices  29.6 us (41%)
  waiting for transfers between devices  25.7 us (36%)
  Pallas kernels  15 us (21%)
  local copies, waits for them, and re-layouts  0.97 us (1%)
    ppermute x14, starting transfers between devices, everyone(): lax.ppermute(message, 'seq', [(i, i ^ by) for i in range(count)])  29.6 us
    ppermute x14, waiting for transfers between devices, everyone(): lax.ppermute(message, 'seq', [(i, i ^ by) for i in range(count)])  25.7 us
    pallas_call x1, Pallas kernels, core_call(): call(functools.partial(core_kernel, blocks, count), 'core', [shape(3 * sl...  9.59 us
    pallas_call x1, Pallas kernels, short_local(): call(tables_kernel, 'tables', [shape(3, TAPS, LANES, dtype=F32), shape(*f...  2.26 us
    pallas_call x1, Pallas kernels, short_local(): call(pack_kernel, 'pack', [shape(6 * slab, LANES)] * count, [scalar] + [a...  1.69 us
  transfers between devices with their start and end apart: 14, of which 6 were waited for; matrix products, arithmetic and copies ran while one was open for 1% of the time, Pallas kernels for 3%

profile of v1, /device:TPU:0, one launch (start us, length us, event | category | flops | bytes accessed | tf_op | source)
XLA Modules:
  0.0 72.0 jit_solution(2973471663217995636)
XLA Ops:
  0.6 1.7 %pack.1 = (bf16[768,128]{1,0:T(8,128)(2,1)S(1)}, bf16[768,128]{1,0:T(8,128)(2,1)S(1)}, bf16[768,128]{1,0:T(8,128)(2,1)S(1)}, bf16[768,128]{1,0:T(8,128)(2,1)S(1)...) custom-call(s32[1]{0:T(128)} %bitcast.me_ref, ...), custom_call_target="tpu_custom_call" | custom-call | tf_op jit(solution)/shard_map/pack/pallas_call | solution.py:442
  2.3 4.0 %collective-permute-start = (bf16[768,128]{1,0:T(8,128)(2,1)S(1)}, bf16[768,128]{1,0:T(8,128)(2,1)S(1)}, u32[]{:S(2)}, u32[]{:S(2)}) collective-permute-start(bf16[768,128]{1,0:T(8,128)(2,1)S(1)} %get-tuple-element.29), channel_id=1, source_target_pairs={{0,6},{2,4},{4,2},{6,0},{8,14},{10,12},{12,10},{14,8},{1,7},{3,5},... | collective-permute-start | bytes 589832 | tf_op jit(solution)/shard_map/ppermute | solution.py:376
  6.3 2.6 %collective-permute-start.1 = (bf16[768,128]{1,0:T(8,128)(2,1)S(1)}, bf16[768,128]{1,0:T(8,128)(2,1)S(1)}, u32[]{:S(2)}, u32[]{:S(2)}) collective-permute-start(bf16[768,128]{1,0:T(8,128)(2,1)S(1)} %get-tuple-element.30), channel_id=1, source_target_pairs={{0,8},{2,10},{4,12},{6,14},{8,0},{10,2},{12,4},{14,6},{1,9},{3,11}... | collective-permute-start | bytes 589832 | tf_op jit(solution)/shard_map/ppermute | solution.py:376
  8.9 0.3 collective-permute-start.2
  9.2 2.5 %collective-permute-start.3 = (bf16[768,128]{1,0:T(8,128)(2,1)S(1)}, bf16[768,128]{1,0:T(8,128)(2,1)S(1)}, u32[]{:S(2)}, u32[]{:S(2)}) collective-permute-start(bf16[768,128]{1,0:T(8,128)(2,1)S(1)} %get-tuple-element.32), channel_id=1, source_target_pairs={{0,12},{2,14},{4,8},{6,10},{8,4},{10,6},{12,0},{14,2},{1,13},{3,15... | collective-permute-start | bytes 589832 | tf_op jit(solution)/shard_map/ppermute | solution.py:376
  11.7 2.3 %collective-permute-start.4 = (bf16[768,128]{1,0:T(8,128)(2,1)S(1)}, bf16[768,128]{1,0:T(8,128)(2,1)S(1)}, u32[]{:S(2)}, u32[]{:S(2)}) collective-permute-start(bf16[768,128]{1,0:T(8,128)(2,1)S(1)} %get-tuple-element.33), channel_id=1, source_target_pairs={{0,14},{2,12},{4,10},{6,8},{8,6},{10,4},{12,2},{14,0},{1,15},{3,13... | collective-permute-start | bytes 589832 | tf_op jit(solution)/shard_map/ppermute | solution.py:376
  14.0 1.3 %collective-permute-done.refs_4_ = bf16[768,128]{1,0:T(8,128)(2,1)S(1)} collective-permute-done((bf16[768,128]{1,0:T(8,128)(2,1)S(1)}, bf16[768,128]{1,0:T(8,128)(2,1)S(1)}, u32[]{:S(2)}, u32[]{:S(2)}) %collective-permute-start) | collective-permute-done | bytes 196640 | tf_op jit(solution)/shard_map/ppermute | solution.py:376
  15.3 0.0 collective-permute-start.5
  15.4 16.6 %collective-permute-done.1.refs_5_ = bf16[768,128]{1,0:T(8,128)(2,1)S(1)} collective-permute-done((bf16[768,128]{1,0:T(8,128)(2,1)S(1)}, bf16[768,128]{1,0:T(8,128)(2,1)S(1)}, u32[]{:S(2)}, u32[]{:S(2)}) %collective-permute-start.1) | collective-permute-done | bytes 196640 | tf_op jit(solution)/shard_map/ppermute | solution.py:376
  31.9 0.3 collective-permute-start.6
  32.3 2.3 %tables.1 = (f32[3,3,128]{2,1,0:T(4,128)S(1)}, bf16[8,512,256]{2,1,0:T(8,128)(2,1)S(1)}, bf16[8,512,256]{2,1,0:T(8,128)(2,1)S(1)}) custom-call(s32[1]{0:T(128)} %bitcast.me_ref, bf16[768,128]{1,0:T(8,128)(2,1)S(1)} %get-tuple-element.25.packed_ref.refs_3_, f32[3,3,1024]{2,1,0:T(4,128)} %refs_10_.1, bf16[8,512,256]{2,1,0:T(8,128)(2,1)} %constant.10.clone.forward_ref, ...), custom_call_target="tpu_custom_call" | custom-call | tf_op jit(solution)/shard_map/tables/pallas_call | solution.py:451
  34.5 1.3 %collective-permute-done.2.refs_6_ = bf16[768,128]{1,0:T(8,128)(2,1)S(1)} collective-permute-done((bf16[768,128]{1,0:T(8,128)(2,1)S(1)}, bf16[768,128]{1,0:T(8,128)(2,1)S(1)}, u32[]{:S(2)}, u32[]{:S(2)}) %collective-permute-start.2) | collective-permute-done | bytes 196640 | tf_op jit(solution)/shard_map/ppermute | solution.py:376
  35.9 0.0 collective-permute-done.3.refs_7_
  35.9 0.0 collective-permute-done.4.refs_8_
  35.9 0.0 collective-permute-done.5.refs_9_
  35.9 1.9 %collective-permute-done.6.refs_10_ = bf16[768,128]{1,0:T(8,128)(2,1)S(1)} collective-permute-done((bf16[768,128]{1,0:T(8,128)(2,1)S(1)}, bf16[768,128]{1,0:T(8,128)(2,1)S(1)}, u32[]{:S(2)}, u32[]{:S(2)}) %collective-permute-start.6) | collective-permute-done | bytes 196640 | tf_op jit(solution)/shard_map/ppermute | solution.py:376
  37.8 0.0 copy-start
  37.8 0.0 copy-start.1
  37.8 9.6 %core.1 = (bf16[432,128]{1,0:T(8,128)(2,1)S(1)}, bf16[432,128]{1,0:T(8,128)(2,1)S(1)}, bf16[432,128]{1,0:T(8,128)(2,1)S(1)}, bf16[432,128]{1,0:T(8,128)(2,1)S(1)...) custom-call(s32[1]{0:T(128)} %bitcast.me_ref, ...), custom_call_target="tpu_custom_call" | custom-call | tf_op jit(solution)/shard_map/core/pallas_call | solution.py:410
  47.4 2.7 %collective-permute-start.10 = (bf16[432,128]{1,0:T(8,128)(2,1)S(1)}, bf16[432,128]{1,0:T(8,128)(2,1)S(1)}, u32[]{:S(2)}, u32[]{:S(2)}) collective-permute-start(bf16[432,128]{1,0:T(8,128)(2,1)S(1)} %get-tuple-element.40), channel_id=1, source_target_pairs={{0,12},{2,14},{4,8},{6,10},{8,4},{10,6},{12,0},{14,2},{1,13},{3,15... | collective-permute-start | bytes 331784 | tf_op jit(solution)/shard_map/ppermute | solution.py:376
  50.1 1.6 %collective-permute-start.11 = (bf16[432,128]{1,0:T(8,128)(2,1)S(1)}, bf16[432,128]{1,0:T(8,128)(2,1)S(1)}, u32[]{:S(2)}, u32[]{:S(2)}) collective-permute-start(bf16[432,128]{1,0:T(8,128)(2,1)S(1)} %get-tuple-element.41), channel_id=1, source_target_pairs={{0,14},{2,12},{4,10},{6,8},{8,6},{10,4},{12,2},{14,0},{1,15},{3,13... | collective-permute-start | bytes 331784 | tf_op jit(solution)/shard_map/ppermute | solution.py:376
  51.8 4.6 %collective-permute-start.12 = (bf16[432,128]{1,0:T(8,128)(2,1)S(1)}, bf16[432,128]{1,0:T(8,128)(2,1)S(1)}, u32[]{:S(2)}, u32[]{:S(2)}) collective-permute-start(bf16[432,128]{1,0:T(8,128)(2,1)S(1)} %get-tuple-element.42), channel_id=1, source_target_pairs={{0,4},{2,6},{4,0},{6,2},{8,12},{10,14},{12,8},{14,10},{1,5},{3,7},... | collective-permute-start | bytes 331784 | tf_op jit(solution)/shard_map/ppermute | solution.py:376
  56.3 0.6 collective-permute-start.13
  56.9 0.9 %collective-permute-start.7 = (bf16[432,128]{1,0:T(8,128)(2,1)S(1)}, bf16[432,128]{1,0:T(8,128)(2,1)S(1)}, u32[]{:S(2)}, u32[]{:S(2)}) collective-permute-start(bf16[432,128]{1,0:T(8,128)(2,1)S(1)} %get-tuple-element.37), channel_id=1, source_target_pairs={{0,6},{2,4},{4,2},{6,0},{8,14},{10,12},{12,10},{14,8},{1,7},{3,5},... | collective-permute-start | bytes 331784 | tf_op jit(solution)/shard_map/ppermute | solution.py:376
  57.8 0.0 collective-permute-done.10.refs_4_
  57.8 3.1 %collective-permute-start.8 = (bf16[432,128]{1,0:T(8,128)(2,1)S(1)}, bf16[432,128]{1,0:T(8,128)(2,1)S(1)}, u32[]{:S(2)}, u32[]{:S(2)}) collective-permute-start(bf16[432,128]{1,0:T(8,128)(2,1)S(1)} %get-tuple-element.38), channel_id=1, source_target_pairs={{0,8},{2,10},{4,12},{6,14},{8,0},{10,2},{12,4},{14,6},{1,9},{3,11}... | collective-permute-start | bytes 331784 | tf_op jit(solution)/shard_map/ppermute | solution.py:376
  60.9 0.0 collective-permute-done.11.refs_5_
  60.9 4.1 %collective-permute-start.9 = (bf16[432,128]{1,0:T(8,128)(2,1)S(1)}, bf16[432,128]{1,0:T(8,128)(2,1)S(1)}, u32[]{:S(2)}, u32[]{:S(2)}) collective-permute-start(bf16[432,128]{1,0:T(8,128)(2,1)S(1)} %get-tuple-element.39), channel_id=1, source_target_pairs={{0,10},{2,8},{4,14},{6,12},{8,2},{10,0},{12,6},{14,4},{1,11},{3,9}... | collective-permute-start | bytes 331784 | tf_op jit(solution)/shard_map/ppermute | solution.py:376
  65.0 1.0 %slice_bitcast_fusion.refs_8_ = bf16[128,1024]{1,0:T(8,128)(2,1)S(1)} fusion(bf16[3,16,8,1024]{3,2,1,0:T(8,128)(2,1)} %param.6), kind=kLoop, calls=%fused_computation | loop fusion | bytes 524288 | tf_op jit(solution)/shard_map/slice | solution.py:475
  66.0 0.0 collective-permute-done.12.refs_6_
  66.0 0.0 collective-permute-done.13.refs_7_
  66.0 0.0 collective-permute-done.7.refs_1_
  66.0 1.7 %collective-permute-done.8.refs_2_ = bf16[432,128]{1,0:T(8,128)(2,1)S(1)} collective-permute-done((bf16[432,128]{1,0:T(8,128)(2,1)S(1)}, bf16[432,128]{1,0:T(8,128)(2,1)S(1)}, u32[]{:S(2)}, u32[]{:S(2)}) %collective-permute-start.8) | collective-permute-done | bytes 110624 | tf_op jit(solution)/shard_map/ppermute | solution.py:376
  67.8 2.8 %collective-permute-done.9.refs_3_ = bf16[432,128]{1,0:T(8,128)(2,1)S(1)} collective-permute-done((bf16[432,128]{1,0:T(8,128)(2,1)S(1)}, bf16[432,128]{1,0:T(8,128)(2,1)S(1)}, u32[]{:S(2)}, u32[]{:S(2)}) %collective-permute-start.9) | collective-permute-done | bytes 110624 | tf_op jit(solution)/shard_map/ppermute | solution.py:376
  70.6 0.0 copy-done
  70.6 0.0 copy-done.1
  70.6 1.4 %home.1 = (bf16[128,1024]{1,0:T(8,128)(2,1)}, bf16[384,1024]{1,0:T(8,128)(2,1)}, f32[3,3,1024]{2,1,0:T(4,128)}) custom-call(s32[1]{0:T(128)} %bitcast.me_ref, bf16[432,128]{1,0:T(8,128)(2,1)S(1)} %get-tuple-element.36.refs_0_, bf16[432,128]{1,0:T(8,128)(2,1)S(1)} %collective-permute-done.7.refs_1_, bf16[432,128]{1,0:T(8,128)(2,1)S(1)} %collective-permute-done.8.refs_2_, ...), custom_call_target="tpu_custom_call" | custom-call | tf_op jit(solution)/shard_map/home/pallas_call | solution.py:466
Async XLA Ops:
  2.3 13.0 %collective-permute-start = (bf16[768,128]{1,0:T(8,128)(2,1)S(1)}, bf16[768,128]{1,0:T(8,128)(2,1)S(1)}, u32[]{:S(2)}, u32[]{:S(2)}) collective-permute-start(bf16[768,128]{1,0:T(8,128)(2,1)S(1)} %get-tuple-element.29), channel_id=1, source_target_pairs={{0,6},{2,4},{4,2},{6,0},{8,14},{10,12},{12,10},{14,8},{1,7},{3,5},... | collective-permute-start | bytes 589832 | tf_op jit(solution)/shard_map/ppermute | solution.py:376
  6.3 25.6 %collective-permute-start.1 = (bf16[768,128]{1,0:T(8,128)(2,1)S(1)}, bf16[768,128]{1,0:T(8,128)(2,1)S(1)}, u32[]{:S(2)}, u32[]{:S(2)}) collective-permute-start(bf16[768,128]{1,0:T(8,128)(2,1)S(1)} %get-tuple-element.30), channel_id=1, source_target_pairs={{0,8},{2,10},{4,12},{6,14},{8,0},{10,2},{12,4},{14,6},{1,9},{3,11}... | collective-permute-start | bytes 589832 | tf_op jit(solution)/shard_map/ppermute | solution.py:376
  8.9 26.9 %collective-permute-start.2 = (bf16[768,128]{1,0:T(8,128)(2,1)S(1)}, bf16[768,128]{1,0:T(8,128)(2,1)S(1)}, u32[]{:S(2)}, u32[]{:S(2)}) collective-permute-start(bf16[768,128]{1,0:T(8,128)(2,1)S(1)} %get-tuple-element.31), channel_id=1, source_target_pairs={{0,10},{2,8},{4,14},{6,12},{8,2},{10,0},{12,6},{14,4},{1,11},{3,9}... | collective-permute-start | bytes 589832 | tf_op jit(solution)/shard_map/ppermute | solution.py:376
  9.2 26.6 %collective-permute-start.3 = (bf16[768,128]{1,0:T(8,128)(2,1)S(1)}, bf16[768,128]{1,0:T(8,128)(2,1)S(1)}, u32[]{:S(2)}, u32[]{:S(2)}) collective-permute-start(bf16[768,128]{1,0:T(8,128)(2,1)S(1)} %get-tuple-element.32), channel_id=1, source_target_pairs={{0,12},{2,14},{4,8},{6,10},{8,4},{10,6},{12,0},{14,2},{1,13},{3,15... | collective-permute-start | bytes 589832 | tf_op jit(solution)/shard_map/ppermute | solution.py:376
  11.7 24.1 %collective-permute-start.4 = (bf16[768,128]{1,0:T(8,128)(2,1)S(1)}, bf16[768,128]{1,0:T(8,128)(2,1)S(1)}, u32[]{:S(2)}, u32[]{:S(2)}) collective-permute-start(bf16[768,128]{1,0:T(8,128)(2,1)S(1)} %get-tuple-element.33), channel_id=1, source_target_pairs={{0,14},{2,12},{4,10},{6,8},{8,6},{10,4},{12,2},{14,0},{1,15},{3,13... | collective-permute-start | bytes 589832 | tf_op jit(solution)/shard_map/ppermute | solution.py:376
  15.3 20.5 %collective-permute-start.5 = (bf16[768,128]{1,0:T(8,128)(2,1)S(1)}, bf16[768,128]{1,0:T(8,128)(2,1)S(1)}, u32[]{:S(2)}, u32[]{:S(2)}) collective-permute-start(bf16[768,128]{1,0:T(8,128)(2,1)S(1)} %get-tuple-element.34), channel_id=1, source_target_pairs={{0,4},{2,6},{4,0},{6,2},{8,12},{10,14},{12,8},{14,10},{1,5},{3,7},... | collective-permute-start | bytes 589832 | tf_op jit(solution)/shard_map/ppermute | solution.py:376
  31.9 5.9 %collective-permute-start.6 = (bf16[768,128]{1,0:T(8,128)(2,1)S(1)}, bf16[768,128]{1,0:T(8,128)(2,1)S(1)}, u32[]{:S(2)}, u32[]{:S(2)}) collective-permute-start(bf16[768,128]{1,0:T(8,128)(2,1)S(1)} %get-tuple-element.35), channel_id=1, source_target_pairs={{0,2},{2,0},{4,6},{6,4},{8,10},{10,8},{12,14},{14,12},{1,3},{3,1},... | collective-permute-start | bytes 589832 | tf_op jit(solution)/shard_map/ppermute | solution.py:376
  37.8 32.8 %copy-start = (bf16[16,8,1024]{2,1,0:T(8,128)(2,1)S(1)}, bf16[16,8,1024]{2,1,0:T(8,128)(2,1)}, u32[]{:S(2)}) copy-start(bf16[16,8,1024]{2,1,0:T(8,128)(2,1)} %param.9) | copy-start | bytes 786436
  37.8 32.8 %copy-start.1 = (f32[3,3,1024]{2,1,0:T(4,128)S(1)}, f32[3,3,1024]{2,1,0:T(4,128)}, u32[]{:S(2)}) copy-start(f32[3,3,1024]{2,1,0:T(4,128)} %refs_10_.1) | copy-start | bytes 110596
  47.4 10.4 %collective-permute-start.10 = (bf16[432,128]{1,0:T(8,128)(2,1)S(1)}, bf16[432,128]{1,0:T(8,128)(2,1)S(1)}, u32[]{:S(2)}, u32[]{:S(2)}) collective-permute-start(bf16[432,128]{1,0:T(8,128)(2,1)S(1)} %get-tuple-element.40), channel_id=1, source_target_pairs={{0,12},{2,14},{4,8},{6,10},{8,4},{10,6},{12,0},{14,2},{1,13},{3,15... | collective-permute-start | bytes 331784 | tf_op jit(solution)/shard_map/ppermute | solution.py:376
  50.1 10.8 %collective-permute-start.11 = (bf16[432,128]{1,0:T(8,128)(2,1)S(1)}, bf16[432,128]{1,0:T(8,128)(2,1)S(1)}, u32[]{:S(2)}, u32[]{:S(2)}) collective-permute-start(bf16[432,128]{1,0:T(8,128)(2,1)S(1)} %get-tuple-element.41), channel_id=1, source_target_pairs={{0,14},{2,12},{4,10},{6,8},{8,6},{10,4},{12,2},{14,0},{1,15},{3,13... | collective-permute-start | bytes 331784 | tf_op jit(solution)/shard_map/ppermute | solution.py:376
  51.8 14.2 %collective-permute-start.12 = (bf16[432,128]{1,0:T(8,128)(2,1)S(1)}, bf16[432,128]{1,0:T(8,128)(2,1)S(1)}, u32[]{:S(2)}, u32[]{:S(2)}) collective-permute-start(bf16[432,128]{1,0:T(8,128)(2,1)S(1)} %get-tuple-element.42), channel_id=1, source_target_pairs={{0,4},{2,6},{4,0},{6,2},{8,12},{10,14},{12,8},{14,10},{1,5},{3,7},... | collective-permute-start | bytes 331784 | tf_op jit(solution)/shard_map/ppermute | solution.py:376
  56.3 9.7 %collective-permute-start.13 = (bf16[432,128]{1,0:T(8,128)(2,1)S(1)}, bf16[432,128]{1,0:T(8,128)(2,1)S(1)}, u32[]{:S(2)}, u32[]{:S(2)}) collective-permute-start(bf16[432,128]{1,0:T(8,128)(2,1)S(1)} %get-tuple-element.43), channel_id=1, source_target_pairs={{0,2},{2,0},{4,6},{6,4},{8,10},{10,8},{12,14},{14,12},{1,3},{3,1},... | collective-permute-start | bytes 331784 | tf_op jit(solution)/shard_map/ppermute | solution.py:376
  56.9 9.1 %collective-permute-start.7 = (bf16[432,128]{1,0:T(8,128)(2,1)S(1)}, bf16[432,128]{1,0:T(8,128)(2,1)S(1)}, u32[]{:S(2)}, u32[]{:S(2)}) collective-permute-start(bf16[432,128]{1,0:T(8,128)(2,1)S(1)} %get-tuple-element.37), channel_id=1, source_target_pairs={{0,6},{2,4},{4,2},{6,0},{8,14},{10,12},{12,10},{14,8},{1,7},{3,5},... | collective-permute-start | bytes 331784 | tf_op jit(solution)/shard_map/ppermute | solution.py:376
  57.8 10.0 %collective-permute-start.8 = (bf16[432,128]{1,0:T(8,128)(2,1)S(1)}, bf16[432,128]{1,0:T(8,128)(2,1)S(1)}, u32[]{:S(2)}, u32[]{:S(2)}) collective-permute-start(bf16[432,128]{1,0:T(8,128)(2,1)S(1)} %get-tuple-element.38), channel_id=1, source_target_pairs={{0,8},{2,10},{4,12},{6,14},{8,0},{10,2},{12,4},{14,6},{1,9},{3,11}... | collective-permute-start | bytes 331784 | tf_op jit(solution)/shard_map/ppermute | solution.py:376
  60.9 9.7 %collective-permute-start.9 = (bf16[432,128]{1,0:T(8,128)(2,1)S(1)}, bf16[432,128]{1,0:T(8,128)(2,1)S(1)}, u32[]{:S(2)}, u32[]{:S(2)}) collective-permute-start(bf16[432,128]{1,0:T(8,128)(2,1)S(1)} %get-tuple-element.39), channel_id=1, source_target_pairs={{0,10},{2,8},{4,14},{6,12},{8,2},{10,0},{12,6},{14,4},{1,11},{3,9}... | collective-permute-start | bytes 331784 | tf_op jit(solution)/shard_map/ppermute | solution.py:376

commit v2 on v1

--- a/solution.py
+++ b/solution.py
@@ -110,18 +110,33 @@
         copy.wait()
 
 
-def pack_kernel(me_ref, streams_ref, filters_ref, grad_ref, *refs):
+def pack_kernel(me_ref, group_ref, streams_ref, filters_ref, grad_ref, *refs):
     outs, sems = refs[:-1], refs[-1]
-    me = me_ref[0]
+    me, group = me_ref[0], group_ref[0]
+    slab = grad_ref.shape[0]
     pairs = []
-    for by, out in zip(sending_order(len(outs)), outs):
+    for by, out in zip(asking_order(len(outs)), outs):
         lanes = pl.ds(pl.multiple_of((me ^ by) * LANES, LANES), LANES)
+        filters = pl.ds(0, 2 * slab)
+        if out.shape[0] == 5 * slab:
+            filters = pl.ds(pl.multiple_of(group * slab, slab), slab)
         at = 0
-        for source in (streams_ref, filters_ref, grad_ref):
+        for source in (
+            streams_ref.at[:, lanes],
+            grad_ref.at[:, lanes],
+            filters_ref.at[filters, lanes],
+        ):
             size = source.shape[0]
-            pairs.append((source.at[:, lanes], out.at[pl.ds(at, size)]))
+            pairs.append((source, out.at[pl.ds(at, size)]))
             at += size
     run_copies(pairs, sems)
+
+
+def swap_kernel(*refs):
+    out = refs[-1]
+    slab = out.shape[0] // (len(refs) - 1)
+    for n, msg in enumerate(refs[:-1]):
+        out[n * slab : (n + 1) * slab] = msg[4 * slab : 5 * slab]
 
 
 def tables_kernel(me_ref, packed_ref, taps_ref, forward_ref, back_ref, *refs):
@@ -197,11 +212,12 @@
     return (now + weights[s, 2:3] * raw[pl.ds(at, size)]).astype(BF16).astype(F32)
 
 
-def core_kernel(blocks, count, me_ref, *refs):
+def core_kernel(blocks, count, me_ref, group_ref, *refs):
     weights, fwd_ref, back_ref = refs[:3]
-    msgs, outs, scratch = refs[3 : 3 + count], refs[3 + count : 3 + 2 * count], refs[3 + 2 * count :]
+    msgs, swapped, refs = refs[3 : 3 + count], refs[3 + count], refs[4 + count :]
+    outs, scratch = refs[:count], refs[count:]
     raw, sig, gate, grad, high, low, spec, turned, cot, conv, grads = scratch
-    me = me_ref[0]
+    me, group = me_ref[0], group_ref[0]
     total = sig.shape[1]
     rows = total // blocks
     slab = total // count
@@ -210,13 +226,20 @@
     def weight(stream, tap):
         return weights[stream, tap : tap + 1]
 
-    for by, msg in zip(sending_order(count), msgs):
+    taken = 0
+    for by, msg in zip(asking_order(count), msgs):
         start = pl.multiple_of((me ^ by) * slab, slab)
         for s in range(3):
             raw[s, pl.ds(halo + start, slab)] = msg[s * slab : (s + 1) * slab].astype(F32)
-        for f in range(2):
-            sig[f, pl.ds(start, slab)] = msg[(3 + f) * slab : (4 + f) * slab].astype(F32)
-        grad[pl.ds(start, slab)] = msg[5 * slab : 6 * slab].astype(F32)
+        grad[pl.ds(start, slab)] = msg[3 * slab : 4 * slab].astype(F32)
+        if msg.shape[0] == 5 * slab:
+            sig[group, pl.ds(start, slab)] = msg[4 * slab :].astype(F32)
+            other = swapped[taken * slab : (taken + 1) * slab]
+            sig[1 - group, pl.ds(start, slab)] = other.astype(F32)
+            taken += 1
+        else:
+            for f in range(2):
+                sig[f, pl.ds(start, slab)] = msg[(4 + f) * slab : (5 + f) * slab].astype(F32)
     for s in range(3):
         raw[s, 0:halo] = shift_blocks(raw[s, total : total + halo], blocks, 1)
 
@@ -316,7 +339,7 @@
     tap_rows = [jnp.sum(part, axis=0, keepdims=True) * scale for part in sums]
     pad = jnp.zeros((TAP_ROWS - 3 * TAPS, LANES), F32)
     tap_block = jnp.concatenate(tap_rows + [pad], axis=0).astype(BF16)
-    for k, by in enumerate(sending_order(count)):
+    for k, by in enumerate(answering_order(count)):
         start = pl.multiple_of((me ^ by) * slab, slab)
         outs[k][0:slab] = conv[pl.ds(start, slab)].astype(BF16)
         for s in range(2):
@@ -344,7 +367,7 @@
     slab = stream_ref.shape[0]
     halo = (TAPS - 1) * blocks
     rest = slab - halo
-    for k, by in enumerate(sending_order(partners)):
+    for k, by in enumerate(answering_order(partners)):
         lanes = pl.ds(pl.multiple_of((me ^ by) * LANES, LANES), LANES)
         msg = msgs[k]
         conv = msg[0:slab].astype(F32)
@@ -364,15 +387,26 @@
             tap_ref[s, :, lanes] = block[s * TAPS : (s + 1) * TAPS]
 
 
-def sending_order(count):
-    far = [k for k in range(1, count) if k > 2]
-    return [0] + far + [k for k in (2, 1) if k < count]
-
-
-def everyone(messages):
+def asking_order(count):
+    half = count // 2
+    near, far = list(range(half - 1, 0, -1)), list(range(half, count))
+    return [0, *far[:1], *near[:1], *far[1:], *near[1:]]
+
+
+def answering_order(count):
+    half = count // 2
+    near, far = list(range(half - 1, 0, -1)), list(range(half, count))
+    return [0, *near[2:], *near[1:2], *far[:1], *near[:1], *far[1:]]
+
+
+def filters_once(count, groups):
+    return [count // 2, count // 2 + 1, count // 2 + 2] if groups == 2 else []
+
+
+def everyone(messages, order):
     count = len(messages)
     out = [messages[0]]
-    for by, message in zip(sending_order(count)[1:], messages[1:]):
+    for by, message in zip(order[1:], messages[1:]):
         out.append(lax.ppermute(message, "seq", [(i, i ^ by) for i in range(count)]))
     return out
 
@@ -401,7 +435,7 @@
     )
 
 
-def core_call(place, tables, messages, blocks):
+def core_call(place, group, tables, messages, swapped, blocks):
     count = len(messages)
     slab = messages[0].shape[0] // 6
     total = slab * count
@@ -411,7 +445,7 @@
         functools.partial(core_kernel, blocks, count),
         "core",
         [shape(3 * slab + 2 * halo + TAP_ROWS, LANES)] * count,
-        [pl.BlockSpec(memory_space=pltpu.SMEM)] + whole_specs(count + 3),
+        [pl.BlockSpec(memory_space=pltpu.SMEM)] * 2 + whole_specs(count + 4),
         [
             pltpu.VMEM((3, halo + total, LANES), F32),
             pltpu.VMEM((4, total, LANES), F32),
@@ -425,12 +459,16 @@
             pltpu.VMEM((total, LANES), F32),
             pltpu.VMEM((2, total, LANES), BF16),
         ],
-    )(place, *tables, *messages)
+    )(place, group, *tables, *messages, swapped)
 
 
 def short_local(streams, short_taps, long_filters, out_grad):
     count = lax.axis_size("seq")
+    groups = lax.axis_size("group")
     place = lax.axis_index("seq").astype(jnp.int32)[None]
+    group = lax.axis_index("group").astype(jnp.int32)[None]
+    order = asking_order(count)
+    once = filters_once(count, groups)
     _, local_rows, blocks, channels = streams.shape
     slab = local_rows * blocks
     flat_streams = streams.reshape(3 * slab, channels)
@@ -442,11 +480,18 @@
     packed = call(
         pack_kernel,
         "pack",
-        [shape(6 * slab, LANES)] * count,
-        [scalar] + [anywhere] * 3,
+        [shape((5 if by in once else 6) * slab, LANES) for by in order],
+        [scalar] * 2 + [anywhere] * 3,
         [pltpu.SemaphoreType.DMA((3 * count,))],
-    )(place, in_hbm(flat_streams), in_hbm(flat_filters), in_hbm(flat_grad))
-    messages = everyone(packed)
+    )(place, group, in_hbm(flat_streams), in_hbm(flat_filters), in_hbm(flat_grad))
+    messages = everyone(packed, order)
+    swapped = jnp.zeros((16, LANES), BF16)
+    if once:
+        halves = [message for by, message in zip(order, messages) if by in once]
+        (mine,) = call(
+            swap_kernel, "swap", [shape(len(once) * slab, LANES)], whole_specs(len(once))
+        )(*halves)
+        swapped = lax.ppermute(mine, "group", [(0, 1), (1, 0)])
     forward, back = transform_tables(blocks, local_rows * count)
     tables = call(
         tables_kernel,
@@ -461,8 +506,8 @@
         in_hbm(jnp.asarray(forward)),
         in_hbm(jnp.asarray(back)),
     )
-    answers = core_call(place, tables, messages, blocks)
-    returned = everyone(answers)
+    answers = core_call(place, group, tables, messages, swapped, blocks)
+    returned = everyone(answers, answering_order(count))
     layer_out, stream_grads, tap_grads = call(
         functools.partial(home_kernel, blocks, count),
         "home",

time: 72.2 us -> 69.5 us (0.963)
  the two profiles are of different devices: /device:TPU:0 before, /device:TPU:16 now
where the time goes in v2:
time: 69.5 us; the launch traced here: 69.3 us
  waiting for transfers between devices  27.7 us (40%)
  starting transfers between devices  25.2 us (36%)
  Pallas kernels  14.7 us (21%)
  local copies, waits for them, and re-layouts  0.98 us (1%)
  between operations  0.73 us (1%)
    ppermute x14, waiting for transfers between devices, everyone(): lax.ppermute(message, 'seq', [(i, i ^ by) for i in range(count)])  27.7 us
    ppermute x14, starting transfers between devices, everyone(): lax.ppermute(message, 'seq', [(i, i ^ by) for i in range(count)])  23.6 us
    pallas_call x1, Pallas kernels, core_call(): call(functools.partial(core_kernel, blocks, count), 'core', [shape(3 * sl...  9.35 us
    pallas_call x1, Pallas kernels, short_local(): call(tables_kernel, 'tables', [shape(3, TAPS, LANES, dtype=F32), shape(*f...  2.26 us
    pallas_call x1, Pallas kernels, short_local(): call(pack_kernel, 'pack', [shape((5 if by in once else 6) * slab, LANES)...  1.66 us
    ppermute x1, starting transfers between devices, short_local(): swapped = lax.ppermute(mine, 'group', [(0, 1), (1, 0)])  1.58 us
    pallas_call x1, Pallas kernels, short_local(): call(functools.partial(home_kernel, blocks, count), 'home', [shape(slab,...  1.43 us
  transfers between devices with their start and end apart: 15, of which 8 were waited for; matrix products, arithmetic and copies ran while one was open for 1% of the time, Pallas kernels for 3%

profile of v2, /device:TPU:16, one launch (start us, length us, event | category | flops | bytes accessed | tf_op | source)
XLA Modules:
  0.0 69.3 jit_solution(8868972473899837160)
XLA Ops:
  0.6 1.7 %pack.1 = (bf16[768,128]{1,0:T(8,128)(2,1)S(1)}, bf16[640,128]{1,0:T(8,128)(2,1)S(1)}, bf16[768,128]{1,0:T(8,128)(2,1)S(1)}, bf16[640,128]{1,0:T(8,128)(2,1)S(1)...) custom-call(s32[1]{0:T(128)} %bitcast.me_ref, ...), custom_call_target="tpu_custom_call" | custom-call | tf_op jit(solution)/shard_map/pack/pallas_call | solution.py:480
  2.3 0.1 collective-permute-start
  2.4 3.8 %collective-permute-start.2 = (bf16[640,128]{1,0:T(8,128)(2,1)S(1)}, bf16[640,128]{1,0:T(8,128)(2,1)S(1)}, u32[]{:S(2)}, u32[]{:S(2)}) collective-permute-start(bf16[640,128]{1,0:T(8,128)(2,1)S(1)} %get-tuple-element.31), channel_id=1, source_target_pairs={{0,10},{2,8},{4,14},{6,12},{8,2},{10,0},{12,6},{14,4},{1,11},{3,9}... | collective-permute-start | bytes 491528 | tf_op jit(solution)/shard_map/ppermute | solution.py:410
  6.2 0.4 collective-permute-start.3
  6.7 1.1 %collective-permute-start.1 = (bf16[768,128]{1,0:T(8,128)(2,1)S(1)}, bf16[768,128]{1,0:T(8,128)(2,1)S(1)}, u32[]{:S(2)}, u32[]{:S(2)}) collective-permute-start(bf16[768,128]{1,0:T(8,128)(2,1)S(1)} %get-tuple-element.30), channel_id=1, source_target_pairs={{0,6},{2,4},{4,2},{6,0},{8,14},{10,12},{12,10},{14,8},{1,7},{3,5},... | collective-permute-start | bytes 589832 | tf_op jit(solution)/shard_map/ppermute | solution.py:410
  7.8 3.8 %collective-permute-start.4 = (bf16[768,128]{1,0:T(8,128)(2,1)S(1)}, bf16[768,128]{1,0:T(8,128)(2,1)S(1)}, u32[]{:S(2)}, u32[]{:S(2)}) collective-permute-start(bf16[768,128]{1,0:T(8,128)(2,1)S(1)} %get-tuple-element.33), channel_id=1, source_target_pairs={{0,14},{2,12},{4,10},{6,8},{8,6},{10,4},{12,2},{14,0},{1,15},{3,13... | collective-permute-start | bytes 589832 | tf_op jit(solution)/shard_map/ppermute | solution.py:410
  11.6 5.9 %collective-permute-done.refs_0_.refs_4_ = bf16[640,128]{1,0:T(8,128)(2,1)S(1)} collective-permute-done((bf16[640,128]{1,0:T(8,128)(2,1)S(1)}, bf16[640,128]{1,0:T(8,128)(2,1)S(1)}, u32[]{:S(2)}, u32[]{:S(2)}) %collective-permute-start) | collective-permute-done | bytes 163872 | tf_op jit(solution)/shard_map/ppermute | solution.py:410
  17.5 4.3 %collective-permute-start.5 = (bf16[768,128]{1,0:T(8,128)(2,1)S(1)}, bf16[768,128]{1,0:T(8,128)(2,1)S(1)}, u32[]{:S(2)}, u32[]{:S(2)}) collective-permute-start(bf16[768,128]{1,0:T(8,128)(2,1)S(1)} %get-tuple-element.34), channel_id=1, source_target_pairs={{0,4},{2,6},{4,0},{6,2},{8,12},{10,14},{12,8},{14,10},{1,5},{3,7},... | collective-permute-start | bytes 589832 | tf_op jit(solution)/shard_map/ppermute | solution.py:410
  21.8 3.5 %collective-permute-done.2.refs_1_.refs_6_ = bf16[640,128]{1,0:T(8,128)(2,1)S(1)} collective-permute-done((bf16[640,128]{1,0:T(8,128)(2,1)S(1)}, bf16[640,128]{1,0:T(8,128)(2,1)S(1)}, u32[]{:S(2)}, u32[]{:S(2)}) %collective-permute-start.2) | collective-permute-done | bytes 163872 | tf_op jit(solution)/shard_map/ppermute | solution.py:410
  25.2 1.8 %collective-permute-start.6 = (bf16[768,128]{1,0:T(8,128)(2,1)S(1)}, bf16[768,128]{1,0:T(8,128)(2,1)S(1)}, u32[]{:S(2)}, u32[]{:S(2)}) collective-permute-start(bf16[768,128]{1,0:T(8,128)(2,1)S(1)} %get-tuple-element.35), channel_id=1, source_target_pairs={{0,2},{2,0},{4,6},{6,4},{8,10},{10,8},{12,14},{14,12},{1,3},{3,1},... | collective-permute-start | bytes 589832 | tf_op jit(solution)/shard_map/ppermute | solution.py:410
  27.1 4.0 %collective-permute-done.3.refs_2_.refs_7_ = bf16[640,128]{1,0:T(8,128)(2,1)S(1)} collective-permute-done((bf16[640,128]{1,0:T(8,128)(2,1)S(1)}, bf16[640,128]{1,0:T(8,128)(2,1)S(1)}, u32[]{:S(2)}, u32[]{:S(2)}) %collective-permute-start.3) | collective-permute-done | bytes 163872 | tf_op jit(solution)/shard_map/ppermute | solution.py:410
  31.1 1.6 %collective-permute-start.7 = (bf16[384,128]{1,0:T(8,128)(2,1)S(1)}, bf16[384,128]{1,0:T(8,128)(2,1)S(1)}, u32[]{:S(2)}, u32[]{:S(2)}) collective-permute-start(bf16[384,128]{1,0:T(8,128)(2,1)S(1)} %swap.1), channel_id=1, source_target_pairs={{0,16},{16,0},{1,17},{17,1},{2,18},{18,2},{3,19},{19,3},{4,20},{20... | collective-permute-start | bytes 294920 | tf_op jit(solution)/shard_map/ppermute | solution.py:494
  32.7 2.3 %tables.1 = (f32[3,3,128]{2,1,0:T(4,128)S(1)}, bf16[8,512,256]{2,1,0:T(8,128)(2,1)S(1)}, bf16[8,512,256]{2,1,0:T(8,128)(2,1)S(1)}) custom-call(s32[1]{0:T(128)} %bitcast.me_ref, bf16[768,128]{1,0:T(8,128)(2,1)S(1)} %get-tuple-element.25.packed_ref.refs_3_, f32[3,3,1024]{2,1,0:T(4,128)} %refs_10_.1, bf16[8,512,256]{2,1,0:T(8,128)(2,1)} %constant.14.clone.forward_ref, ...), custom_call_target="tpu_custom_call" | custom-call | tf_op jit(solution)/shard_map/tables/pallas_call | solution.py:496
  35.0 0.0 collective-permute-done.1.refs_5_
  35.0 1.2 %collective-permute-done.4.refs_8_ = bf16[768,128]{1,0:T(8,128)(2,1)S(1)} collective-permute-done((bf16[768,128]{1,0:T(8,128)(2,1)S(1)}, bf16[768,128]{1,0:T(8,128)(2,1)S(1)}, u32[]{:S(2)}, u32[]{:S(2)}) %collective-permute-start.4) | collective-permute-done | bytes 196640 | tf_op jit(solution)/shard_map/ppermute | solution.py:410
  36.2 0.0 collective-permute-done.5.refs_9_
  36.2 0.0 collective-permute-done.6.refs_10_
  36.2 0.0 collective-permute-done.7.refs_11_
  36.2 0.0 copy-start
  36.2 0.0 copy-start.1
  36.2 9.3 %core.1 = (bf16[432,128]{1,0:T(8,128)(2,1)S(1)}, bf16[432,128]{1,0:T(8,128)(2,1)S(1)}, bf16[432,128]{1,0:T(8,128)(2,1)S(1)}, bf16[432,128]{1,0:T(8,128)(2,1)S(1)...) custom-call(s32[1]{0:T(128)} %bitcast.me_ref, ...), custom_call_target="tpu_custom_call" | custom-call | tf_op jit(solution)/shard_map/core/pallas_call | solution.py:444
  45.5 0.1 collective-permute-start.10
  45.6 4.2 %collective-permute-start.11 = (bf16[432,128]{1,0:T(8,128)(2,1)S(1)}, bf16[432,128]{1,0:T(8,128)(2,1)S(1)}, u32[]{:S(2)}, u32[]{:S(2)}) collective-permute-start(bf16[432,128]{1,0:T(8,128)(2,1)S(1)} %get-tuple-element.40), channel_id=1, source_target_pairs={{0,6},{2,4},{4,2},{6,0},{8,14},{10,12},{12,10},{14,8},{1,7},{3,5},... | collective-permute-start | bytes 331784 | tf_op jit(solution)/shard_map/ppermute | solution.py:410
  49.8 0.1 collective-permute-start.12
  50.0 1.3 %collective-permute-start.13 = (bf16[432,128]{1,0:T(8,128)(2,1)S(1)}, bf16[432,128]{1,0:T(8,128)(2,1)S(1)}, u32[]{:S(2)}, u32[]{:S(2)}) collective-permute-start(bf16[432,128]{1,0:T(8,128)(2,1)S(1)} %get-tuple-element.42), channel_id=1, source_target_pairs={{0,12},{2,14},{4,8},{6,10},{8,4},{10,6},{12,0},{14,2},{1,13},{3,15... | collective-permute-start | bytes 331784 | tf_op jit(solution)/shard_map/ppermute | solution.py:410
  51.3 1.5 %collective-permute-start.14 = (bf16[432,128]{1,0:T(8,128)(2,1)S(1)}, bf16[432,128]{1,0:T(8,128)(2,1)S(1)}, u32[]{:S(2)}, u32[]{:S(2)}) collective-permute-start(bf16[432,128]{1,0:T(8,128)(2,1)S(1)} %get-tuple-element.43), channel_id=1, source_target_pairs={{0,14},{2,12},{4,10},{6,8},{8,6},{10,4},{12,2},{14,0},{1,15},{3,13... | collective-permute-start | bytes 331784 | tf_op jit(solution)/shard_map/ppermute | solution.py:410
  52.8 0.0 collective-permute-done.10.refs_3_
  52.8 0.6 collective-permute-start.8
  53.5 3.0 %collective-permute-done.11.refs_4_ = bf16[432,128]{1,0:T(8,128)(2,1)S(1)} collective-permute-done((bf16[432,128]{1,0:T(8,128)(2,1)S(1)}, bf16[432,128]{1,0:T(8,128)(2,1)S(1)}, u32[]{:S(2)}, u32[]{:S(2)}) %collective-permute-start.11) | collective-permute-done | bytes 110624 | tf_op jit(solution)/shard_map/ppermute | solution.py:410
  56.4 0.3 collective-permute-start.9
  56.8 1.0 %slice_bitcast_fusion.refs_8_ = bf16[128,1024]{1,0:T(8,128)(2,1)S(1)} fusion(bf16[3,16,8,1024]{3,2,1,0:T(8,128)(2,1)} %param.6), kind=kLoop, calls=%fused_computation | loop fusion | bytes 524288 | tf_op jit(solution)/shard_map/slice | solution.py:520
  57.7 2.5 %collective-permute-done.12.refs_5_ = bf16[432,128]{1,0:T(8,128)(2,1)S(1)} collective-permute-done((bf16[432,128]{1,0:T(8,128)(2,1)S(1)}, bf16[432,128]{1,0:T(8,128)(2,1)S(1)}, u32[]{:S(2)}, u32[]{:S(2)}) %collective-permute-start.12) | collective-permute-done | bytes 110624 | tf_op jit(solution)/shard_map/ppermute | solution.py:410
  60.2 5.2 %collective-permute-done.13.refs_6_ = bf16[432,128]{1,0:T(8,128)(2,1)S(1)} collective-permute-done((bf16[432,128]{1,0:T(8,128)(2,1)S(1)}, bf16[432,128]{1,0:T(8,128)(2,1)S(1)}, u32[]{:S(2)}, u32[]{:S(2)}) %collective-permute-start.13) | collective-permute-done | bytes 110624 | tf_op jit(solution)/shard_map/ppermute | solution.py:410
  65.4 2.4 %collective-permute-done.14.refs_7_ = bf16[432,128]{1,0:T(8,128)(2,1)S(1)} collective-permute-done((bf16[432,128]{1,0:T(8,128)(2,1)S(1)}, bf16[432,128]{1,0:T(8,128)(2,1)S(1)}, u32[]{:S(2)}, u32[]{:S(2)}) %collective-permute-start.14) | collective-permute-done | bytes 110624 | tf_op jit(solution)/shard_map/ppermute | solution.py:410
  67.8 0.0 collective-permute-done.8.refs_1_
  67.8 0.0 collective-permute-done.9.refs_2_
  67.8 0.0 copy-done
  67.8 0.0 copy-done.1
  67.9 1.4 %home.1 = (bf16[128,1024]{1,0:T(8,128)(2,1)}, bf16[384,1024]{1,0:T(8,128)(2,1)}, f32[3,3,1024]{2,1,0:T(4,128)}) custom-call(s32[1]{0:T(128)} %bitcast.me_ref, bf16[432,128]{1,0:T(8,128)(2,1)S(1)} %get-tuple-element.36.refs_0_, bf16[432,128]{1,0:T(8,128)(2,1)S(1)} %collective-permute-done.8.refs_1_, bf16[432,128]{1,0:T(8,128)(2,1)S(1)} %collective-permute-done.9.refs_2_, ...), custom_call_target="tpu_custom_call" | custom-call | tf_op jit(solution)/shard_map/home/pallas_call | solution.py:511
  (1 shorter events, 0.0 us)
Async XLA Ops:
  2.3 15.2 %collective-permute-start = (bf16[640,128]{1,0:T(8,128)(2,1)S(1)}, bf16[640,128]{1,0:T(8,128)(2,1)S(1)}, u32[]{:S(2)}, u32[]{:S(2)}) collective-permute-start(bf16[640,128]{1,0:T(8,128)(2,1)S(1)} %get-tuple-element.29), channel_id=1, source_target_pairs={{0,8},{2,10},{4,12},{6,14},{8,0},{10,2},{12,4},{14,6},{1,9},{3,11}... | collective-permute-start | bytes 491528 | tf_op jit(solution)/shard_map/ppermute | solution.py:410
  2.4 22.9 %collective-permute-start.2 = (bf16[640,128]{1,0:T(8,128)(2,1)S(1)}, bf16[640,128]{1,0:T(8,128)(2,1)S(1)}, u32[]{:S(2)}, u32[]{:S(2)}) collective-permute-start(bf16[640,128]{1,0:T(8,128)(2,1)S(1)} %get-tuple-element.31), channel_id=1, source_target_pairs={{0,10},{2,8},{4,14},{6,12},{8,2},{10,0},{12,6},{14,4},{1,11},{3,9}... | collective-permute-start | bytes 491528 | tf_op jit(solution)/shard_map/ppermute | solution.py:410
  6.2 24.9 %collective-permute-start.3 = (bf16[640,128]{1,0:T(8,128)(2,1)S(1)}, bf16[640,128]{1,0:T(8,128)(2,1)S(1)}, u32[]{:S(2)}, u32[]{:S(2)}) collective-permute-start(bf16[640,128]{1,0:T(8,128)(2,1)S(1)} %get-tuple-element.32), channel_id=1, source_target_pairs={{0,12},{2,14},{4,8},{6,10},{8,4},{10,6},{12,0},{14,2},{1,13},{3,15... | collective-permute-start | bytes 491528 | tf_op jit(solution)/shard_map/ppermute | solution.py:410
  6.7 28.3 %collective-permute-start.1 = (bf16[768,128]{1,0:T(8,128)(2,1)S(1)}, bf16[768,128]{1,0:T(8,128)(2,1)S(1)}, u32[]{:S(2)}, u32[]{:S(2)}) collective-permute-start(bf16[768,128]{1,0:T(8,128)(2,1)S(1)} %get-tuple-element.30), channel_id=1, source_target_pairs={{0,6},{2,4},{4,2},{6,0},{8,14},{10,12},{12,10},{14,8},{1,7},{3,5},... | collective-permute-start | bytes 589832 | tf_op jit(solution)/shard_map/ppermute | solution.py:410
  7.8 28.4 %collective-permute-start.4 = (bf16[768,128]{1,0:T(8,128)(2,1)S(1)}, bf16[768,128]{1,0:T(8,128)(2,1)S(1)}, u32[]{:S(2)}, u32[]{:S(2)}) collective-permute-start(bf16[768,128]{1,0:T(8,128)(2,1)S(1)} %get-tuple-element.33), channel_id=1, source_target_pairs={{0,14},{2,12},{4,10},{6,8},{8,6},{10,4},{12,2},{14,0},{1,15},{3,13... | collective-permute-start | bytes 589832 | tf_op jit(solution)/shard_map/ppermute | solution.py:410
  17.5 18.6 %collective-permute-start.5 = (bf16[768,128]{1,0:T(8,128)(2,1)S(1)}, bf16[768,128]{1,0:T(8,128)(2,1)S(1)}, u32[]{:S(2)}, u32[]{:S(2)}) collective-permute-start(bf16[768,128]{1,0:T(8,128)(2,1)S(1)} %get-tuple-element.34), channel_id=1, source_target_pairs={{0,4},{2,6},{4,0},{6,2},{8,12},{10,14},{12,8},{14,10},{1,5},{3,7},... | collective-permute-start | bytes 589832 | tf_op jit(solution)/shard_map/ppermute | solution.py:410
  25.2 10.9 %collective-permute-start.6 = (bf16[768,128]{1,0:T(8,128)(2,1)S(1)}, bf16[768,128]{1,0:T(8,128)(2,1)S(1)}, u32[]{:S(2)}, u32[]{:S(2)}) collective-permute-start(bf16[768,128]{1,0:T(8,128)(2,1)S(1)} %get-tuple-element.35), channel_id=1, source_target_pairs={{0,2},{2,0},{4,6},{6,4},{8,10},{10,8},{12,14},{14,12},{1,3},{3,1},... | collective-permute-start | bytes 589832 | tf_op jit(solution)/shard_map/ppermute | solution.py:410
  31.1 5.0 %collective-permute-start.7 = (bf16[384,128]{1,0:T(8,128)(2,1)S(1)}, bf16[384,128]{1,0:T(8,128)(2,1)S(1)}, u32[]{:S(2)}, u32[]{:S(2)}) collective-permute-start(bf16[384,128]{1,0:T(8,128)(2,1)S(1)} %swap.1), channel_id=1, source_target_pairs={{0,16},{16,0},{1,17},{17,1},{2,18},{18,2},{3,19},{19,3},{4,20},{20... | collective-permute-start | bytes 294920 | tf_op jit(solution)/shard_map/ppermute | solution.py:494
  36.2 31.7 %copy-start = (bf16[16,8,1024]{2,1,0:T(8,128)(2,1)S(1)}, bf16[16,8,1024]{2,1,0:T(8,128)(2,1)}, u32[]{:S(2)}) copy-start(bf16[16,8,1024]{2,1,0:T(8,128)(2,1)} %param.9) | copy-start | bytes 786436
  36.2 31.7 %copy-start.1 = (f32[3,3,1024]{2,1,0:T(4,128)S(1)}, f32[3,3,1024]{2,1,0:T(4,128)}, u32[]{:S(2)}) copy-start(f32[3,3,1024]{2,1,0:T(4,128)} %refs_10_.1) | copy-start | bytes 110596
  45.5 7.3 %collective-permute-start.10 = (bf16[432,128]{1,0:T(8,128)(2,1)S(1)}, bf16[432,128]{1,0:T(8,128)(2,1)S(1)}, u32[]{:S(2)}, u32[]{:S(2)}) collective-permute-start(bf16[432,128]{1,0:T(8,128)(2,1)S(1)} %get-tuple-element.39), channel_id=1, source_target_pairs={{0,8},{2,10},{4,12},{6,14},{8,0},{10,2},{12,4},{14,6},{1,9},{3,11}... | collective-permute-start | bytes 331784 | tf_op jit(solution)/shard_map/ppermute | solution.py:410
  45.6 10.8 %collective-permute-start.11 = (bf16[432,128]{1,0:T(8,128)(2,1)S(1)}, bf16[432,128]{1,0:T(8,128)(2,1)S(1)}, u32[]{:S(2)}, u32[]{:S(2)}) collective-permute-start(bf16[432,128]{1,0:T(8,128)(2,1)S(1)} %get-tuple-element.40), channel_id=1, source_target_pairs={{0,6},{2,4},{4,2},{6,0},{8,14},{10,12},{12,10},{14,8},{1,7},{3,5},... | collective-permute-start | bytes 331784 | tf_op jit(solution)/shard_map/ppermute | solution.py:410
  49.8 10.4 %collective-permute-start.12 = (bf16[432,128]{1,0:T(8,128)(2,1)S(1)}, bf16[432,128]{1,0:T(8,128)(2,1)S(1)}, u32[]{:S(2)}, u32[]{:S(2)}) collective-permute-start(bf16[432,128]{1,0:T(8,128)(2,1)S(1)} %get-tuple-element.41), channel_id=1, source_target_pairs={{0,10},{2,8},{4,14},{6,12},{8,2},{10,0},{12,6},{14,4},{1,11},{3,9}... | collective-permute-start | bytes 331784 | tf_op jit(solution)/shard_map/ppermute | solution.py:410
  50.0 15.5 %collective-permute-start.13 = (bf16[432,128]{1,0:T(8,128)(2,1)S(1)}, bf16[432,128]{1,0:T(8,128)(2,1)S(1)}, u32[]{:S(2)}, u32[]{:S(2)}) collective-permute-start(bf16[432,128]{1,0:T(8,128)(2,1)S(1)} %get-tuple-element.42), channel_id=1, source_target_pairs={{0,12},{2,14},{4,8},{6,10},{8,4},{10,6},{12,0},{14,2},{1,13},{3,15... | collective-permute-start | bytes 331784 | tf_op jit(solution)/shard_map/ppermute | solution.py:410
  51.3 16.5 %collective-permute-start.14 = (bf16[432,128]{1,0:T(8,128)(2,1)S(1)}, bf16[432,128]{1,0:T(8,128)(2,1)S(1)}, u32[]{:S(2)}, u32[]{:S(2)}) collective-permute-start(bf16[432,128]{1,0:T(8,128)(2,1)S(1)} %get-tuple-element.43), channel_id=1, source_target_pairs={{0,14},{2,12},{4,10},{6,8},{8,6},{10,4},{12,2},{14,0},{1,15},{3,13... | collective-permute-start | bytes 331784 | tf_op jit(solution)/shard_map/ppermute | solution.py:410
  52.8 15.0 %collective-permute-start.8 = (bf16[432,128]{1,0:T(8,128)(2,1)S(1)}, bf16[432,128]{1,0:T(8,128)(2,1)S(1)}, u32[]{:S(2)}, u32[]{:S(2)}) collective-permute-start(bf16[432,128]{1,0:T(8,128)(2,1)S(1)} %get-tuple-element.37), channel_id=1, source_target_pairs={{0,2},{2,0},{4,6},{6,4},{8,10},{10,8},{12,14},{14,12},{1,3},{3,1},... | collective-permute-start | bytes 331784 | tf_op jit(solution)/shard_map/ppermute | solution.py:410
  56.4 11.4 %collective-permute-start.9 = (bf16[432,128]{1,0:T(8,128)(2,1)S(1)}, bf16[432,128]{1,0:T(8,128)(2,1)S(1)}, u32[]{:S(2)}, u32[]{:S(2)}) collective-permute-start(bf16[432,128]{1,0:T(8,128)(2,1)S(1)} %get-tuple-element.38), channel_id=1, source_target_pairs={{0,4},{2,6},{4,0},{6,2},{8,12},{10,14},{12,8},{14,10},{1,5},{3,7},... | collective-permute-start | bytes 331784 | tf_op jit(solution)/shard_map/ppermute | solution.py:410

commit v3 on v2

--- a/solution.py
+++ b/solution.py
@@ -388,19 +388,15 @@
 
 
 def asking_order(count):
-    half = count // 2
-    near, far = list(range(half - 1, 0, -1)), list(range(half, count))
-    return [0, *far[:1], *near[:1], *far[1:], *near[1:]]
+    return [0, 4, 3, 2, 5, 6, 7, 1] if count == 8 else list(range(count))
 
 
 def answering_order(count):
-    half = count // 2
-    near, far = list(range(half - 1, 0, -1)), list(range(half, count))
-    return [0, *near[2:], *near[1:2], *far[:1], *near[:1], *far[1:]]
+    return [0, 1, 2, 4, 3, 5, 7, 6] if count == 8 else list(range(count))
 
 
 def filters_once(count, groups):
-    return [count // 2, count // 2 + 1, count // 2 + 2] if groups == 2 else []
+    return list(range(count // 2, count - 1)) if groups == 2 else []
 
 
 def everyone(messages, order):

time: 69.5 us -> 67.9 us (0.977)
  the two profiles are of different devices: /device:TPU:16 before, /device:TPU:0 now
where the time goes in v3:
time: 67.9 us; the launch traced here: 67.7 us
  starting transfers between devices  28.9 us (43%)
  waiting for transfers between devices  22.4 us (33%)
  Pallas kernels  14.7 us (22%)
  local copies, waits for them, and re-layouts  0.97 us (1%)
  between operations  0.68 us (1%)
    ppermute x14, starting transfers between devices, everyone(): lax.ppermute(message, 'seq', [(i, i ^ by) for i in range(count)])  27 us
    ppermute x14, waiting for transfers between devices, everyone(): lax.ppermute(message, 'seq', [(i, i ^ by) for i in range(count)])  22.4 us
    pallas_call x1, Pallas kernels, core_call(): call(functools.partial(core_kernel, blocks, count), 'core', [shape(3 * sl...  9.34 us
    pallas_call x1, Pallas kernels, short_local(): call(tables_kernel, 'tables', [shape(3, TAPS, LANES, dtype=F32), shape(*f...  2.26 us
    ppermute x1, starting transfers between devices, short_local(): swapped = lax.ppermute(mine, 'group', [(0, 1), (1, 0)])  1.93 us
    pallas_call x1, Pallas kernels, short_local(): call(pack_kernel, 'pack', [shape((5 if by in once else 6) * slab, LANES)...  1.66 us
    pallas_call x1, Pallas kernels, short_local(): call(functools.partial(home_kernel, blocks, count), 'home', [shape(slab,...  1.43 us
  transfers between devices with their start and end apart: 15, of which 8 were waited for; matrix products, arithmetic and copies ran while one was open for 1% of the time, Pallas kernels for 3%

profile of v3, /device:TPU:0, one launch (start us, length us, event | category | flops | bytes accessed | tf_op | source)
XLA Modules:
  0.0 67.7 jit_solution(6806533912096667787)
XLA Ops:
  0.6 1.7 %pack.1 = (bf16[768,128]{1,0:T(8,128)(2,1)S(1)}, bf16[640,128]{1,0:T(8,128)(2,1)S(1)}, bf16[768,128]{1,0:T(8,128)(2,1)S(1)}, bf16[768,128]{1,0:T(8,128)(2,1)S(1)...) custom-call(s32[1]{0:T(128)} %bitcast.me_ref, ...), custom_call_target="tpu_custom_call" | custom-call | tf_op jit(solution)/shard_map/pack/pallas_call | solution.py:476
  2.3 4.1 %collective-permute-start = (bf16[640,128]{1,0:T(8,128)(2,1)S(1)}, bf16[640,128]{1,0:T(8,128)(2,1)S(1)}, u32[]{:S(2)}, u32[]{:S(2)}) collective-permute-start(bf16[640,128]{1,0:T(8,128)(2,1)S(1)} %get-tuple-element.29), channel_id=1, source_target_pairs={{0,8},{2,10},{4,12},{6,14},{8,0},{10,2},{12,4},{14,6},{1,9},{3,11}... | collective-permute-start | bytes 491528 | tf_op jit(solution)/shard_map/ppermute | solution.py:406
  6.4 1.3 %collective-permute-start.3 = (bf16[640,128]{1,0:T(8,128)(2,1)S(1)}, bf16[640,128]{1,0:T(8,128)(2,1)S(1)}, u32[]{:S(2)}, u32[]{:S(2)}) collective-permute-start(bf16[640,128]{1,0:T(8,128)(2,1)S(1)} %get-tuple-element.32), channel_id=1, source_target_pairs={{0,10},{2,8},{4,14},{6,12},{8,2},{10,0},{12,6},{14,4},{1,11},{3,9}... | collective-permute-start | bytes 491528 | tf_op jit(solution)/shard_map/ppermute | solution.py:406
  7.7 3.6 %collective-permute-start.4 = (bf16[640,128]{1,0:T(8,128)(2,1)S(1)}, bf16[640,128]{1,0:T(8,128)(2,1)S(1)}, u32[]{:S(2)}, u32[]{:S(2)}) collective-permute-start(bf16[640,128]{1,0:T(8,128)(2,1)S(1)} %get-tuple-element.33), channel_id=1, source_target_pairs={{0,12},{2,14},{4,8},{6,10},{8,4},{10,6},{12,0},{14,2},{1,13},{3,15... | collective-permute-start | bytes 491528 | tf_op jit(solution)/shard_map/ppermute | solution.py:406
  11.3 0.0 collective-permute-start.1
  11.3 2.0 %collective-permute-start.2 = (bf16[768,128]{1,0:T(8,128)(2,1)S(1)}, bf16[768,128]{1,0:T(8,128)(2,1)S(1)}, u32[]{:S(2)}, u32[]{:S(2)}) collective-permute-start(bf16[768,128]{1,0:T(8,128)(2,1)S(1)} %get-tuple-element.31), channel_id=1, source_target_pairs={{0,4},{2,6},{4,0},{6,2},{8,12},{10,14},{12,8},{14,10},{1,5},{3,7},... | collective-permute-start | bytes 589832 | tf_op jit(solution)/shard_map/ppermute | solution.py:406
  13.3 8.8 %collective-permute-done.refs_0_.refs_4_ = bf16[640,128]{1,0:T(8,128)(2,1)S(1)} collective-permute-done((bf16[640,128]{1,0:T(8,128)(2,1)S(1)}, bf16[640,128]{1,0:T(8,128)(2,1)S(1)}, u32[]{:S(2)}, u32[]{:S(2)}) %collective-permute-start) | collective-permute-done | bytes 163872 | tf_op jit(solution)/shard_map/ppermute | solution.py:406
  22.1 3.7 %collective-permute-start.5 = (bf16[768,128]{1,0:T(8,128)(2,1)S(1)}, bf16[768,128]{1,0:T(8,128)(2,1)S(1)}, u32[]{:S(2)}, u32[]{:S(2)}) collective-permute-start(bf16[768,128]{1,0:T(8,128)(2,1)S(1)} %get-tuple-element.34), channel_id=1, source_target_pairs={{0,14},{2,12},{4,10},{6,8},{8,6},{10,4},{12,2},{14,0},{1,15},{3,13... | collective-permute-start | bytes 589832 | tf_op jit(solution)/shard_map/ppermute | solution.py:406
  25.8 1.0 %collective-permute-done.3.refs_1_.refs_7_ = bf16[640,128]{1,0:T(8,128)(2,1)S(1)} collective-permute-done((bf16[640,128]{1,0:T(8,128)(2,1)S(1)}, bf16[640,128]{1,0:T(8,128)(2,1)S(1)}, u32[]{:S(2)}, u32[]{:S(2)}) %collective-permute-start.3) | collective-permute-done | bytes 163872 | tf_op jit(solution)/shard_map/ppermute | solution.py:406
  26.8 0.2 collective-permute-start.6
  27.0 0.0 collective-permute-done.4.refs_2_.refs_8_
  27.0 1.9 %collective-permute-start.7 = (bf16[384,128]{1,0:T(8,128)(2,1)S(1)}, bf16[384,128]{1,0:T(8,128)(2,1)S(1)}, u32[]{:S(2)}, u32[]{:S(2)}) collective-permute-start(bf16[384,128]{1,0:T(8,128)(2,1)S(1)} %swap.1), channel_id=1, source_target_pairs={{0,16},{16,0},{1,17},{17,1},{2,18},{18,2},{3,19},{19,3},{4,20},{20... | collective-permute-start | bytes 294920 | tf_op jit(solution)/shard_map/ppermute | solution.py:490
  28.9 2.3 %tables.1 = (f32[3,3,128]{2,1,0:T(4,128)S(1)}, bf16[8,512,256]{2,1,0:T(8,128)(2,1)S(1)}, bf16[8,512,256]{2,1,0:T(8,128)(2,1)S(1)}) custom-call(s32[1]{0:T(128)} %bitcast.me_ref, bf16[768,128]{1,0:T(8,128)(2,1)S(1)} %get-tuple-element.25.packed_ref.refs_3_, f32[3,3,1024]{2,1,0:T(4,128)} %refs_10_.1, bf16[8,512,256]{2,1,0:T(8,128)(2,1)} %constant.14.clone.forward_ref, ...), custom_call_target="tpu_custom_call" | custom-call | tf_op jit(solution)/shard_map/tables/pallas_call | solution.py:492
  31.2 2.1 %collective-permute-done.1.refs_5_ = bf16[768,128]{1,0:T(8,128)(2,1)S(1)} collective-permute-done((bf16[768,128]{1,0:T(8,128)(2,1)S(1)}, bf16[768,128]{1,0:T(8,128)(2,1)S(1)}, u32[]{:S(2)}, u32[]{:S(2)}) %collective-permute-start.1) | collective-permute-done | bytes 196640 | tf_op jit(solution)/shard_map/ppermute | solution.py:406
  33.3 1.5 %collective-permute-done.2.refs_6_ = bf16[768,128]{1,0:T(8,128)(2,1)S(1)} collective-permute-done((bf16[768,128]{1,0:T(8,128)(2,1)S(1)}, bf16[768,128]{1,0:T(8,128)(2,1)S(1)}, u32[]{:S(2)}, u32[]{:S(2)}) %collective-permute-start.2) | collective-permute-done | bytes 196640 | tf_op jit(solution)/shard_map/ppermute | solution.py:406
  34.8 0.0 collective-permute-done.5.refs_9_
  34.8 1.9 %collective-permute-done.6.refs_10_ = bf16[768,128]{1,0:T(8,128)(2,1)S(1)} collective-permute-done((bf16[768,128]{1,0:T(8,128)(2,1)S(1)}, bf16[768,128]{1,0:T(8,128)(2,1)S(1)}, u32[]{:S(2)}, u32[]{:S(2)}) %collective-permute-start.6) | collective-permute-done | bytes 196640 | tf_op jit(solution)/shard_map/ppermute | solution.py:406
  36.7 0.0 collective-permute-done.7.refs_11_
  36.7 0.0 copy-start
  36.7 0.0 copy-start.1
  36.7 9.3 %core.1 = (bf16[432,128]{1,0:T(8,128)(2,1)S(1)}, bf16[432,128]{1,0:T(8,128)(2,1)S(1)}, bf16[432,128]{1,0:T(8,128)(2,1)S(1)}, bf16[432,128]{1,0:T(8,128)(2,1)S(1)...) custom-call(s32[1]{0:T(128)} %bitcast.me_ref, ...), custom_call_target="tpu_custom_call" | custom-call | tf_op jit(solution)/shard_map/core/pallas_call | solution.py:440
  46.1 3.6 %collective-permute-start.10 = (bf16[432,128]{1,0:T(8,128)(2,1)S(1)}, bf16[432,128]{1,0:T(8,128)(2,1)S(1)}, u32[]{:S(2)}, u32[]{:S(2)}) collective-permute-start(bf16[432,128]{1,0:T(8,128)(2,1)S(1)} %get-tuple-element.39), channel_id=1, source_target_pairs={{0,8},{2,10},{4,12},{6,14},{8,0},{10,2},{12,4},{14,6},{1,9},{3,11}... | collective-permute-start | bytes 331784 | tf_op jit(solution)/shard_map/ppermute | solution.py:406
  49.6 0.0 collective-permute-start.11
  49.6 2.1 %collective-permute-start.12 = (bf16[432,128]{1,0:T(8,128)(2,1)S(1)}, bf16[432,128]{1,0:T(8,128)(2,1)S(1)}, u32[]{:S(2)}, u32[]{:S(2)}) collective-permute-start(bf16[432,128]{1,0:T(8,128)(2,1)S(1)} %get-tuple-element.41), channel_id=1, source_target_pairs={{0,10},{2,8},{4,14},{6,12},{8,2},{10,0},{12,6},{14,4},{1,11},{3,9}... | collective-permute-start | bytes 331784 | tf_op jit(solution)/shard_map/ppermute | solution.py:406
  51.7 3.7 %collective-permute-start.13 = (bf16[432,128]{1,0:T(8,128)(2,1)S(1)}, bf16[432,128]{1,0:T(8,128)(2,1)S(1)}, u32[]{:S(2)}, u32[]{:S(2)}) collective-permute-start(bf16[432,128]{1,0:T(8,128)(2,1)S(1)} %get-tuple-element.42), channel_id=1, source_target_pairs={{0,14},{2,12},{4,10},{6,8},{8,6},{10,4},{12,2},{14,0},{1,15},{3,13... | collective-permute-start | bytes 331784 | tf_op jit(solution)/shard_map/ppermute | solution.py:406
  55.5 1.4 %collective-permute-start.14 = (bf16[432,128]{1,0:T(8,128)(2,1)S(1)}, bf16[432,128]{1,0:T(8,128)(2,1)S(1)}, u32[]{:S(2)}, u32[]{:S(2)}) collective-permute-start(bf16[432,128]{1,0:T(8,128)(2,1)S(1)} %get-tuple-element.43), channel_id=1, source_target_pairs={{0,12},{2,14},{4,8},{6,10},{8,4},{10,6},{12,0},{14,2},{1,13},{3,15... | collective-permute-start | bytes 331784 | tf_op jit(solution)/shard_map/ppermute | solution.py:406
  56.8 0.0 collective-permute-done.10.refs_3_
  56.8 0.2 collective-permute-start.8
  57.0 0.4 collective-permute-done.11.refs_4_
  57.4 1.2 %collective-permute-start.9 = (bf16[432,128]{1,0:T(8,128)(2,1)S(1)}, bf16[432,128]{1,0:T(8,128)(2,1)S(1)}, u32[]{:S(2)}, u32[]{:S(2)}) collective-permute-start(bf16[432,128]{1,0:T(8,128)(2,1)S(1)} %get-tuple-element.38), channel_id=1, source_target_pairs={{0,4},{2,6},{4,0},{6,2},{8,12},{10,14},{12,8},{14,10},{1,5},{3,7},... | collective-permute-start | bytes 331784 | tf_op jit(solution)/shard_map/ppermute | solution.py:406
  58.6 1.0 %slice_bitcast_fusion.refs_8_ = bf16[128,1024]{1,0:T(8,128)(2,1)S(1)} fusion(bf16[3,16,8,1024]{3,2,1,0:T(8,128)(2,1)} %param.6), kind=kLoop, calls=%fused_computation | loop fusion | bytes 524288 | tf_op jit(solution)/shard_map/slice | solution.py:516
  59.6 5.4 %collective-permute-done.12.refs_5_ = bf16[432,128]{1,0:T(8,128)(2,1)S(1)} collective-permute-done((bf16[432,128]{1,0:T(8,128)(2,1)S(1)}, bf16[432,128]{1,0:T(8,128)(2,1)S(1)}, u32[]{:S(2)}, u32[]{:S(2)}) %collective-permute-start.12) | collective-permute-done | bytes 110624 | tf_op jit(solution)/shard_map/ppermute | solution.py:406
  65.0 0.0 collective-permute-done.13.refs_6_
  65.0 0.0 collective-permute-done.14.refs_7_
  65.0 0.0 collective-permute-done.8.refs_1_
  65.0 1.3 %collective-permute-done.9.refs_2_ = bf16[432,128]{1,0:T(8,128)(2,1)S(1)} collective-permute-done((bf16[432,128]{1,0:T(8,128)(2,1)S(1)}, bf16[432,128]{1,0:T(8,128)(2,1)S(1)}, u32[]{:S(2)}, u32[]{:S(2)}) %collective-permute-start.9) | collective-permute-done | bytes 110624 | tf_op jit(solution)/shard_map/ppermute | solution.py:406
  66.2 0.0 copy-done
  66.2 0.0 copy-done.1
  66.3 1.4 %home.1 = (bf16[128,1024]{1,0:T(8,128)(2,1)}, bf16[384,1024]{1,0:T(8,128)(2,1)}, f32[3,3,1024]{2,1,0:T(4,128)}) custom-call(s32[1]{0:T(128)} %bitcast.me_ref, bf16[432,128]{1,0:T(8,128)(2,1)S(1)} %get-tuple-element.36.refs_0_, bf16[432,128]{1,0:T(8,128)(2,1)S(1)} %collective-permute-done.8.refs_1_, bf16[432,128]{1,0:T(8,128)(2,1)S(1)} %collective-permute-done.9.refs_2_, ...), custom_call_target="tpu_custom_call" | custom-call | tf_op jit(solution)/shard_map/home/pallas_call | solution.py:507
  (1 shorter events, 0.0 us)
Async XLA Ops:
  2.3 19.8 %collective-permute-start = (bf16[640,128]{1,0:T(8,128)(2,1)S(1)}, bf16[640,128]{1,0:T(8,128)(2,1)S(1)}, u32[]{:S(2)}, u32[]{:S(2)}) collective-permute-start(bf16[640,128]{1,0:T(8,128)(2,1)S(1)} %get-tuple-element.29), channel_id=1, source_target_pairs={{0,8},{2,10},{4,12},{6,14},{8,0},{10,2},{12,4},{14,6},{1,9},{3,11}... | collective-permute-start | bytes 491528 | tf_op jit(solution)/shard_map/ppermute | solution.py:406
  6.4 20.4 %collective-permute-start.3 = (bf16[640,128]{1,0:T(8,128)(2,1)S(1)}, bf16[640,128]{1,0:T(8,128)(2,1)S(1)}, u32[]{:S(2)}, u32[]{:S(2)}) collective-permute-start(bf16[640,128]{1,0:T(8,128)(2,1)S(1)} %get-tuple-element.32), channel_id=1, source_target_pairs={{0,10},{2,8},{4,14},{6,12},{8,2},{10,0},{12,6},{14,4},{1,11},{3,9}... | collective-permute-start | bytes 491528 | tf_op jit(solution)/shard_map/ppermute | solution.py:406
  7.7 19.3 %collective-permute-start.4 = (bf16[640,128]{1,0:T(8,128)(2,1)S(1)}, bf16[640,128]{1,0:T(8,128)(2,1)S(1)}, u32[]{:S(2)}, u32[]{:S(2)}) collective-permute-start(bf16[640,128]{1,0:T(8,128)(2,1)S(1)} %get-tuple-element.33), channel_id=1, source_target_pairs={{0,12},{2,14},{4,8},{6,10},{8,4},{10,6},{12,0},{14,2},{1,13},{3,15... | collective-permute-start | bytes 491528 | tf_op jit(solution)/shard_map/ppermute | solution.py:406
  11.3 22.1 %collective-permute-start.1 = (bf16[768,128]{1,0:T(8,128)(2,1)S(1)}, bf16[768,128]{1,0:T(8,128)(2,1)S(1)}, u32[]{:S(2)}, u32[]{:S(2)}) collective-permute-start(bf16[768,128]{1,0:T(8,128)(2,1)S(1)} %get-tuple-element.30), channel_id=1, source_target_pairs={{0,6},{2,4},{4,2},{6,0},{8,14},{10,12},{12,10},{14,8},{1,7},{3,5},... | collective-permute-start | bytes 589832 | tf_op jit(solution)/shard_map/ppermute | solution.py:406
  11.3 23.6 %collective-permute-start.2 = (bf16[768,128]{1,0:T(8,128)(2,1)S(1)}, bf16[768,128]{1,0:T(8,128)(2,1)S(1)}, u32[]{:S(2)}, u32[]{:S(2)}) collective-permute-start(bf16[768,128]{1,0:T(8,128)(2,1)S(1)} %get-tuple-element.31), channel_id=1, source_target_pairs={{0,4},{2,6},{4,0},{6,2},{8,12},{10,14},{12,8},{14,10},{1,5},{3,7},... | collective-permute-start | bytes 589832 | tf_op jit(solution)/shard_map/ppermute | solution.py:406
  22.1 12.8 %collective-permute-start.5 = (bf16[768,128]{1,0:T(8,128)(2,1)S(1)}, bf16[768,128]{1,0:T(8,128)(2,1)S(1)}, u32[]{:S(2)}, u32[]{:S(2)}) collective-permute-start(bf16[768,128]{1,0:T(8,128)(2,1)S(1)} %get-tuple-element.34), channel_id=1, source_target_pairs={{0,14},{2,12},{4,10},{6,8},{8,6},{10,4},{12,2},{14,0},{1,15},{3,13... | collective-permute-start | bytes 589832 | tf_op jit(solution)/shard_map/ppermute | solution.py:406
  26.8 9.9 %collective-permute-start.6 = (bf16[768,128]{1,0:T(8,128)(2,1)S(1)}, bf16[768,128]{1,0:T(8,128)(2,1)S(1)}, u32[]{:S(2)}, u32[]{:S(2)}) collective-permute-start(bf16[768,128]{1,0:T(8,128)(2,1)S(1)} %get-tuple-element.35), channel_id=1, source_target_pairs={{0,2},{2,0},{4,6},{6,4},{8,10},{10,8},{12,14},{14,12},{1,3},{3,1},... | collective-permute-start | bytes 589832 | tf_op jit(solution)/shard_map/ppermute | solution.py:406
  27.0 9.7 %collective-permute-start.7 = (bf16[384,128]{1,0:T(8,128)(2,1)S(1)}, bf16[384,128]{1,0:T(8,128)(2,1)S(1)}, u32[]{:S(2)}, u32[]{:S(2)}) collective-permute-start(bf16[384,128]{1,0:T(8,128)(2,1)S(1)} %swap.1), channel_id=1, source_target_pairs={{0,16},{16,0},{1,17},{17,1},{2,18},{18,2},{3,19},{19,3},{4,20},{20... | collective-permute-start | bytes 294920 | tf_op jit(solution)/shard_map/ppermute | solution.py:490
  36.7 29.5 %copy-start = (bf16[16,8,1024]{2,1,0:T(8,128)(2,1)S(1)}, bf16[16,8,1024]{2,1,0:T(8,128)(2,1)}, u32[]{:S(2)}) copy-start(bf16[16,8,1024]{2,1,0:T(8,128)(2,1)} %param.9) | copy-start | bytes 786436
  36.7 29.5 %copy-start.1 = (f32[3,3,1024]{2,1,0:T(4,128)S(1)}, f32[3,3,1024]{2,1,0:T(4,128)}, u32[]{:S(2)}) copy-start(f32[3,3,1024]{2,1,0:T(4,128)} %refs_10_.1) | copy-start | bytes 110596
  46.1 10.8 %collective-permute-start.10 = (bf16[432,128]{1,0:T(8,128)(2,1)S(1)}, bf16[432,128]{1,0:T(8,128)(2,1)S(1)}, u32[]{:S(2)}, u32[]{:S(2)}) collective-permute-start(bf16[432,128]{1,0:T(8,128)(2,1)S(1)} %get-tuple-element.39), channel_id=1, source_target_pairs={{0,8},{2,10},{4,12},{6,14},{8,0},{10,2},{12,4},{14,6},{1,9},{3,11}... | collective-permute-start | bytes 331784 | tf_op jit(solution)/shard_map/ppermute | solution.py:406
  49.6 7.8 %collective-permute-start.11 = (bf16[432,128]{1,0:T(8,128)(2,1)S(1)}, bf16[432,128]{1,0:T(8,128)(2,1)S(1)}, u32[]{:S(2)}, u32[]{:S(2)}) collective-permute-start(bf16[432,128]{1,0:T(8,128)(2,1)S(1)} %get-tuple-element.40), channel_id=1, source_target_pairs={{0,6},{2,4},{4,2},{6,0},{8,14},{10,12},{12,10},{14,8},{1,7},{3,5},... | collective-permute-start | bytes 331784 | tf_op jit(solution)/shard_map/ppermute | solution.py:406
  49.6 15.3 %collective-permute-start.12 = (bf16[432,128]{1,0:T(8,128)(2,1)S(1)}, bf16[432,128]{1,0:T(8,128)(2,1)S(1)}, u32[]{:S(2)}, u32[]{:S(2)}) collective-permute-start(bf16[432,128]{1,0:T(8,128)(2,1)S(1)} %get-tuple-element.41), channel_id=1, source_target_pairs={{0,10},{2,8},{4,14},{6,12},{8,2},{10,0},{12,6},{14,4},{1,11},{3,9}... | collective-permute-start | bytes 331784 | tf_op jit(solution)/shard_map/ppermute | solution.py:406
  51.7 13.2 %collective-permute-start.13 = (bf16[432,128]{1,0:T(8,128)(2,1)S(1)}, bf16[432,128]{1,0:T(8,128)(2,1)S(1)}, u32[]{:S(2)}, u32[]{:S(2)}) collective-permute-start(bf16[432,128]{1,0:T(8,128)(2,1)S(1)} %get-tuple-element.42), channel_id=1, source_target_pairs={{0,14},{2,12},{4,10},{6,8},{8,6},{10,4},{12,2},{14,0},{1,15},{3,13... | collective-permute-start | bytes 331784 | tf_op jit(solution)/shard_map/ppermute | solution.py:406
  55.5 9.5 %collective-permute-start.14 = (bf16[432,128]{1,0:T(8,128)(2,1)S(1)}, bf16[432,128]{1,0:T(8,128)(2,1)S(1)}, u32[]{:S(2)}, u32[]{:S(2)}) collective-permute-start(bf16[432,128]{1,0:T(8,128)(2,1)S(1)} %get-tuple-element.43), channel_id=1, source_target_pairs={{0,12},{2,14},{4,8},{6,10},{8,4},{10,6},{12,0},{14,2},{1,13},{3,15... | collective-permute-start | bytes 331784 | tf_op jit(solution)/shard_map/ppermute | solution.py:406
  56.8 8.1 %collective-permute-start.8 = (bf16[432,128]{1,0:T(8,128)(2,1)S(1)}, bf16[432,128]{1,0:T(8,128)(2,1)S(1)}, u32[]{:S(2)}, u32[]{:S(2)}) collective-permute-start(bf16[432,128]{1,0:T(8,128)(2,1)S(1)} %get-tuple-element.37), channel_id=1, source_target_pairs={{0,2},{2,0},{4,6},{6,4},{8,10},{10,8},{12,14},{14,12},{1,3},{3,1},... | collective-permute-start | bytes 331784 | tf_op jit(solution)/shard_map/ppermute | solution.py:406
  57.4 8.8 %collective-permute-start.9 = (bf16[432,128]{1,0:T(8,128)(2,1)S(1)}, bf16[432,128]{1,0:T(8,128)(2,1)S(1)}, u32[]{:S(2)}, u32[]{:S(2)}) collective-permute-start(bf16[432,128]{1,0:T(8,128)(2,1)S(1)} %get-tuple-element.38), channel_id=1, source_target_pairs={{0,4},{2,6},{4,0},{6,2},{8,12},{10,14},{12,8},{14,10},{1,5},{3,7},... | collective-permute-start | bytes 331784 | tf_op jit(solution)/shard_map/ppermute | solution.py:406

commit v4 on v3

--- a/solution.py
+++ b/solution.py
@@ -110,25 +110,31 @@
         copy.wait()
 
 
+def message_pairs(out, lanes, group, streams_ref, filters_ref, grad_ref):
+    slab = grad_ref.shape[0]
+    filters = pl.ds(0, 2 * slab)
+    if out.shape[0] == 5 * slab:
+        filters = pl.ds(pl.multiple_of(group * slab, slab), slab)
+    sources = (
+        streams_ref.at[:, lanes],
+        grad_ref.at[:, lanes],
+        filters_ref.at[filters, lanes],
+    )
+    at, pairs = 0, []
+    for source in sources:
+        size = source.shape[0]
+        pairs.append((source, out.at[pl.ds(at, size)]))
+        at += size
+    return pairs
+
+
 def pack_kernel(me_ref, group_ref, streams_ref, filters_ref, grad_ref, *refs):
     outs, sems = refs[:-1], refs[-1]
     me, group = me_ref[0], group_ref[0]
-    slab = grad_ref.shape[0]
     pairs = []
-    for by, out in zip(asking_order(len(outs)), outs):
+    for by, out in zip(asking_order(len(outs) + 1)[1:], outs):
         lanes = pl.ds(pl.multiple_of((me ^ by) * LANES, LANES), LANES)
-        filters = pl.ds(0, 2 * slab)
-        if out.shape[0] == 5 * slab:
-            filters = pl.ds(pl.multiple_of(group * slab, slab), slab)
-        at = 0
-        for source in (
-            streams_ref.at[:, lanes],
-            grad_ref.at[:, lanes],
-            filters_ref.at[filters, lanes],
-        ):
-            size = source.shape[0]
-            pairs.append((source, out.at[pl.ds(at, size)]))
-            at += size
+        pairs += message_pairs(out, lanes, group, streams_ref, filters_ref, grad_ref)
     run_copies(pairs, sems)
 
 
@@ -141,10 +147,11 @@
 
 def tables_kernel(me_ref, packed_ref, taps_ref, forward_ref, back_ref, *refs):
     del packed_ref
-    outs, sems = refs[:-1], refs[-1]
+    arrays, outs, sems = refs[:3], refs[3:-1], refs[-1]
     lanes = pl.ds(pl.multiple_of(me_ref[0] * LANES, LANES), LANES)
     sources = (taps_ref.at[:, :, lanes], forward_ref, back_ref)
-    run_copies(zip(sources, outs), sems)
+    pairs = list(zip(sources, outs)) + message_pairs(outs[3], lanes, None, *arrays)
+    run_copies(pairs, sems)
 
 
 class Transforms:
@@ -266,16 +273,12 @@
         if j < steps:
             butterflies(j * CHUNK, (2, 3))
 
-    def forward_data(j):
-        turned[j] = work.forward(j, 2 * LANES, 4 * LANES)
-
     def first_products(j):
-        data = turned[j]
+        data = work.forward(j, 2 * LANES, 4 * LANES)
         left = product(data[:, :LANES], spec[j, :, :LANES])
         right = product(data[:, LANES:], spec[j, :, LANES:], True)
         turned[j] = work.backward(j, jnp.concatenate([left, right], axis=1))
 
-    work.each_slot(forward_data)
     work.each_slot(first_products)
 
     def gates(row):
@@ -476,11 +479,29 @@
     packed = call(
         pack_kernel,
         "pack",
-        [shape((5 if by in once else 6) * slab, LANES) for by in order],
+        [shape((5 if by in once else 6) * slab, LANES) for by in order[1:]],
         [scalar] * 2 + [anywhere] * 3,
-        [pltpu.SemaphoreType.DMA((3 * count,))],
+        [pltpu.SemaphoreType.DMA((3 * (count - 1),))],
     )(place, group, in_hbm(flat_streams), in_hbm(flat_filters), in_hbm(flat_grad))
-    messages = everyone(packed, order)
+    forward, back = transform_tables(blocks, local_rows * count)
+    *tables, own = call(
+        tables_kernel,
+        "tables",
+        [shape(3, TAPS, LANES, dtype=F32), shape(*forward.shape), shape(*back.shape)]
+        + [shape(6 * slab, LANES)],
+        [scalar] + [anywhere] * 7,
+        [pltpu.SemaphoreType.DMA((6,))],
+    )(
+        place,
+        packed[0],
+        in_hbm(short_taps),
+        in_hbm(jnp.asarray(forward)),
+        in_hbm(jnp.asarray(back)),
+        in_hbm(flat_streams),
+        in_hbm(flat_filters),
+        in_hbm(flat_grad),
+    )
+    messages = everyone([own, *packed], order)
     swapped = jnp.zeros((16, LANES), BF16)
     if once:
         halves = [message for by, message in zip(order, messages) if by in once]
@@ -488,20 +509,6 @@
             swap_kernel, "swap", [shape(len(once) * slab, LANES)], whole_specs(len(once))
         )(*halves)
         swapped = lax.ppermute(mine, "group", [(0, 1), (1, 0)])
-    forward, back = transform_tables(blocks, local_rows * count)
-    tables = call(
-        tables_kernel,
-        "tables",
-        [shape(3, TAPS, LANES, dtype=F32), shape(*forward.shape), shape(*back.shape)],
-        [scalar] + [anywhere] * 4,
-        [pltpu.SemaphoreType.DMA((3,))],
-    )(
-        place,
-        packed[0],
-        in_hbm(short_taps),
-        in_hbm(jnp.asarray(forward)),
-        in_hbm(jnp.asarray(back)),
-    )
     answers = core_call(place, group, tables, messages, swapped, blocks)
     returned = everyone(answers, answering_order(count))
     layer_out, stream_grads, tap_grads = call(

time: 67.9 us -> 67.9 us (level)
  no operation moved by 1% of the time
where the time goes in v4:
time: 67.9 us; the launch traced here: 67.7 us
  starting transfers between devices  28.9 us (43%)
  waiting for transfers between devices  22.4 us (33%)
  Pallas kernels  14.7 us (22%)
  local copies, waits for them, and re-layouts  0.97 us (1%)
  between operations  0.68 us (1%)
    ppermute x14, starting transfers between devices, everyone(): lax.ppermute(message, 'seq', [(i, i ^ by) for i in range(count)])  27 us
    ppermute x14, waiting for transfers between devices, everyone(): lax.ppermute(message, 'seq', [(i, i ^ by) for i in range(count)])  22.4 us
    pallas_call x1, Pallas kernels, core_call(): call(functools.partial(core_kernel, blocks, count), 'core', [shape(3 * sl...  9.41 us
    pallas_call x1, Pallas kernels, short_local(): call(tables_kernel, 'tables', [shape(3, TAPS, LANES, dtype=F32), shape(*f...  2.29 us
    ppermute x1, starting transfers between devices, short_local(): swapped = lax.ppermute(mine, 'group', [(0, 1), (1, 0)])  1.93 us
    pallas_call x1, Pallas kernels, short_local(): call(pack_kernel, 'pack', [shape((5 if by in once else 6) * slab, LANES)...  1.57 us
    pallas_call x1, Pallas kernels, short_local(): call(functools.partial(home_kernel, blocks, count), 'home', [shape(slab,...  1.43 us
  transfers between devices with their start and end apart: 15, of which 8 were waited for; matrix products, arithmetic and copies ran while one was open for 1% of the time, Pallas kernels for 3%

profile of v4, /device:TPU:0, one launch (start us, length us, event | category | flops | bytes accessed | tf_op | source)
XLA Modules:
  0.0 67.7 jit_solution(5935430952196680683)
XLA Ops:
  0.6 1.6 %pack.1 = (bf16[640,128]{1,0:T(8,128)(2,1)S(1)}, bf16[768,128]{1,0:T(8,128)(2,1)S(1)}, bf16[768,128]{1,0:T(8,128)(2,1)S(1)}, bf16[640,128]{1,0:T(8,128)(2,1)S(1)...) custom-call(s32[1]{0:T(128)} %bitcast.me_ref, s32[1]{0:T(128)} %bitcast.1.group_ref, ...), custom_call_target="tpu_custom_call" | custom-call | tf_op jit(solution)/shard_map/pack/pallas_call | solution.py:479
  2.2 4.1 %collective-permute-start = (bf16[640,128]{1,0:T(8,128)(2,1)S(1)}, bf16[640,128]{1,0:T(8,128)(2,1)S(1)}, u32[]{:S(2)}, u32[]{:S(2)}) collective-permute-start(bf16[640,128]{1,0:T(8,128)(2,1)S(1)} %get-tuple-element.25.packed_ref), channel_id=1, source_target_pairs={{0,8},{2,10},{4,12},{6,14},{8,0},{10,2},{12,4},{14,6},{1,9},{3,11}... | collective-permute-start | bytes 491528 | tf_op jit(solution)/shard_map/ppermute | solution.py:409
  6.3 1.3 %collective-permute-start.3 = (bf16[640,128]{1,0:T(8,128)(2,1)S(1)}, bf16[640,128]{1,0:T(8,128)(2,1)S(1)}, u32[]{:S(2)}, u32[]{:S(2)}) collective-permute-start(bf16[640,128]{1,0:T(8,128)(2,1)S(1)} %get-tuple-element.32), channel_id=1, source_target_pairs={{0,10},{2,8},{4,14},{6,12},{8,2},{10,0},{12,6},{14,4},{1,11},{3,9}... | collective-permute-start | bytes 491528 | tf_op jit(solution)/shard_map/ppermute | solution.py:409
  7.6 3.6 %collective-permute-start.4 = (bf16[640,128]{1,0:T(8,128)(2,1)S(1)}, bf16[640,128]{1,0:T(8,128)(2,1)S(1)}, u32[]{:S(2)}, u32[]{:S(2)}) collective-permute-start(bf16[640,128]{1,0:T(8,128)(2,1)S(1)} %get-tuple-element.33), channel_id=1, source_target_pairs={{0,12},{2,14},{4,8},{6,10},{8,4},{10,6},{12,0},{14,2},{1,13},{3,15... | collective-permute-start | bytes 491528 | tf_op jit(solution)/shard_map/ppermute | solution.py:409
  11.2 0.0 collective-permute-start.1
  11.2 2.0 %collective-permute-start.2 = (bf16[768,128]{1,0:T(8,128)(2,1)S(1)}, bf16[768,128]{1,0:T(8,128)(2,1)S(1)}, u32[]{:S(2)}, u32[]{:S(2)}) collective-permute-start(bf16[768,128]{1,0:T(8,128)(2,1)S(1)} %get-tuple-element.31), channel_id=1, source_target_pairs={{0,4},{2,6},{4,0},{6,2},{8,12},{10,14},{12,8},{14,10},{1,5},{3,7},... | collective-permute-start | bytes 589832 | tf_op jit(solution)/shard_map/ppermute | solution.py:409
  13.2 8.8 %collective-permute-done.refs_0_.refs_4_ = bf16[640,128]{1,0:T(8,128)(2,1)S(1)} collective-permute-done((bf16[640,128]{1,0:T(8,128)(2,1)S(1)}, bf16[640,128]{1,0:T(8,128)(2,1)S(1)}, u32[]{:S(2)}, u32[]{:S(2)}) %collective-permute-start) | collective-permute-done | bytes 163872 | tf_op jit(solution)/shard_map/ppermute | solution.py:409
  22.0 3.7 %collective-permute-start.5 = (bf16[768,128]{1,0:T(8,128)(2,1)S(1)}, bf16[768,128]{1,0:T(8,128)(2,1)S(1)}, u32[]{:S(2)}, u32[]{:S(2)}) collective-permute-start(bf16[768,128]{1,0:T(8,128)(2,1)S(1)} %get-tuple-element.34), channel_id=1, source_target_pairs={{0,14},{2,12},{4,10},{6,8},{8,6},{10,4},{12,2},{14,0},{1,15},{3,13... | collective-permute-start | bytes 589832 | tf_op jit(solution)/shard_map/ppermute | solution.py:409
  25.7 1.0 %collective-permute-done.3.refs_1_.refs_7_ = bf16[640,128]{1,0:T(8,128)(2,1)S(1)} collective-permute-done((bf16[640,128]{1,0:T(8,128)(2,1)S(1)}, bf16[640,128]{1,0:T(8,128)(2,1)S(1)}, u32[]{:S(2)}, u32[]{:S(2)}) %collective-permute-start.3) | collective-permute-done | bytes 163872 | tf_op jit(solution)/shard_map/ppermute | solution.py:409
  26.7 0.2 collective-permute-start.6
  26.9 0.0 collective-permute-done.4.refs_2_.refs_8_
  26.9 1.9 %collective-permute-start.7 = (bf16[384,128]{1,0:T(8,128)(2,1)S(1)}, bf16[384,128]{1,0:T(8,128)(2,1)S(1)}, u32[]{:S(2)}, u32[]{:S(2)}) collective-permute-start(bf16[384,128]{1,0:T(8,128)(2,1)S(1)} %swap.1), channel_id=1, source_target_pairs={{0,16},{16,0},{1,17},{17,1},{2,18},{18,2},{3,19},{19,3},{4,20},{20... | collective-permute-start | bytes 294920 | tf_op jit(solution)/shard_map/ppermute | solution.py:511
  28.8 2.3 %tables.1 = (f32[3,3,128]{2,1,0:T(4,128)S(1)}, bf16[8,512,256]{2,1,0:T(8,128)(2,1)S(1)}, bf16[8,512,256]{2,1,0:T(8,128)(2,1)S(1)}, bf16[768,128]{1,0:T(8,128)(2,1)S(1)}) custom-call(s32[1]{0:T(128)} %bitcast.me_ref, bf16[640,128]{1,0:T(8,128)(2,1)S(1)} %get-tuple-element.25.packed_ref, f32[3,3,1024]{2,1,0:T(4,128)} %refs_10_.1, ...), custom_call_target="tpu_custom_call" | custom-call | tf_op jit(solution)/shard_map/tables/pallas_call | solution.py:487
  31.1 2.1 %collective-permute-done.1.refs_5_ = bf16[768,128]{1,0:T(8,128)(2,1)S(1)} collective-permute-done((bf16[768,128]{1,0:T(8,128)(2,1)S(1)}, bf16[768,128]{1,0:T(8,128)(2,1)S(1)}, u32[]{:S(2)}, u32[]{:S(2)}) %collective-permute-start.1) | collective-permute-done | bytes 196640 | tf_op jit(solution)/shard_map/ppermute | solution.py:409
  33.2 1.5 %collective-permute-done.2.refs_6_ = bf16[768,128]{1,0:T(8,128)(2,1)S(1)} collective-permute-done((bf16[768,128]{1,0:T(8,128)(2,1)S(1)}, bf16[768,128]{1,0:T(8,128)(2,1)S(1)}, u32[]{:S(2)}, u32[]{:S(2)}) %collective-permute-start.2) | collective-permute-done | bytes 196640 | tf_op jit(solution)/shard_map/ppermute | solution.py:409
  34.7 0.0 collective-permute-done.5.refs_9_
  34.7 1.9 %collective-permute-done.6.refs_10_ = bf16[768,128]{1,0:T(8,128)(2,1)S(1)} collective-permute-done((bf16[768,128]{1,0:T(8,128)(2,1)S(1)}, bf16[768,128]{1,0:T(8,128)(2,1)S(1)}, u32[]{:S(2)}, u32[]{:S(2)}) %collective-permute-start.6) | collective-permute-done | bytes 196640 | tf_op jit(solution)/shard_map/ppermute | solution.py:409
  36.6 0.0 collective-permute-done.7.refs_11_
  36.6 0.0 copy-start
  36.6 0.0 copy-start.1
  36.6 9.4 %core.1 = (bf16[432,128]{1,0:T(8,128)(2,1)S(1)}, bf16[432,128]{1,0:T(8,128)(2,1)S(1)}, bf16[432,128]{1,0:T(8,128)(2,1)S(1)}, bf16[432,128]{1,0:T(8,128)(2,1)S(1)...) custom-call(s32[1]{0:T(128)} %bitcast.me_ref, ...), custom_call_target="tpu_custom_call" | custom-call | tf_op jit(solution)/shard_map/core/pallas_call | solution.py:443
  46.0 3.6 %collective-permute-start.10 = (bf16[432,128]{1,0:T(8,128)(2,1)S(1)}, bf16[432,128]{1,0:T(8,128)(2,1)S(1)}, u32[]{:S(2)}, u32[]{:S(2)}) collective-permute-start(bf16[432,128]{1,0:T(8,128)(2,1)S(1)} %get-tuple-element.39), channel_id=1, source_target_pairs={{0,8},{2,10},{4,12},{6,14},{8,0},{10,2},{12,4},{14,6},{1,9},{3,11}... | collective-permute-start | bytes 331784 | tf_op jit(solution)/shard_map/ppermute | solution.py:409
  49.6 0.0 collective-permute-start.11
  49.6 2.1 %collective-permute-start.12 = (bf16[432,128]{1,0:T(8,128)(2,1)S(1)}, bf16[432,128]{1,0:T(8,128)(2,1)S(1)}, u32[]{:S(2)}, u32[]{:S(2)}) collective-permute-start(bf16[432,128]{1,0:T(8,128)(2,1)S(1)} %get-tuple-element.41), channel_id=1, source_target_pairs={{0,10},{2,8},{4,14},{6,12},{8,2},{10,0},{12,6},{14,4},{1,11},{3,9}... | collective-permute-start | bytes 331784 | tf_op jit(solution)/shard_map/ppermute | solution.py:409
  51.7 3.7 %collective-permute-start.13 = (bf16[432,128]{1,0:T(8,128)(2,1)S(1)}, bf16[432,128]{1,0:T(8,128)(2,1)S(1)}, u32[]{:S(2)}, u32[]{:S(2)}) collective-permute-start(bf16[432,128]{1,0:T(8,128)(2,1)S(1)} %get-tuple-element.42), channel_id=1, source_target_pairs={{0,14},{2,12},{4,10},{6,8},{8,6},{10,4},{12,2},{14,0},{1,15},{3,13... | collective-permute-start | bytes 331784 | tf_op jit(solution)/shard_map/ppermute | solution.py:409
  55.4 1.4 %collective-permute-start.14 = (bf16[432,128]{1,0:T(8,128)(2,1)S(1)}, bf16[432,128]{1,0:T(8,128)(2,1)S(1)}, u32[]{:S(2)}, u32[]{:S(2)}) collective-permute-start(bf16[432,128]{1,0:T(8,128)(2,1)S(1)} %get-tuple-element.43), channel_id=1, source_target_pairs={{0,12},{2,14},{4,8},{6,10},{8,4},{10,6},{12,0},{14,2},{1,13},{3,15... | collective-permute-start | bytes 331784 | tf_op jit(solution)/shard_map/ppermute | solution.py:409
  56.8 0.0 collective-permute-done.10.refs_3_
  56.8 0.2 collective-permute-start.8
  57.0 0.4 collective-permute-done.11.refs_4_
  57.4 1.2 %collective-permute-start.9 = (bf16[432,128]{1,0:T(8,128)(2,1)S(1)}, bf16[432,128]{1,0:T(8,128)(2,1)S(1)}, u32[]{:S(2)}, u32[]{:S(2)}) collective-permute-start(bf16[432,128]{1,0:T(8,128)(2,1)S(1)} %get-tuple-element.38), channel_id=1, source_target_pairs={{0,4},{2,6},{4,0},{6,2},{8,12},{10,14},{12,8},{14,10},{1,5},{3,7},... | collective-permute-start | bytes 331784 | tf_op jit(solution)/shard_map/ppermute | solution.py:409
  58.6 1.0 %slice_bitcast_fusion.refs_8_ = bf16[128,1024]{1,0:T(8,128)(2,1)S(1)} fusion(bf16[3,16,8,1024]{3,2,1,0:T(8,128)(2,1)} %param.6), kind=kLoop, calls=%fused_computation | loop fusion | bytes 524288 | tf_op jit(solution)/shard_map/slice | solution.py:523
  59.5 5.4 %collective-permute-done.12.refs_5_ = bf16[432,128]{1,0:T(8,128)(2,1)S(1)} collective-permute-done((bf16[432,128]{1,0:T(8,128)(2,1)S(1)}, bf16[432,128]{1,0:T(8,128)(2,1)S(1)}, u32[]{:S(2)}, u32[]{:S(2)}) %collective-permute-start.12) | collective-permute-done | bytes 110624 | tf_op jit(solution)/shard_map/ppermute | solution.py:409
  64.9 0.0 collective-permute-done.13.refs_6_
  64.9 0.0 collective-permute-done.14.refs_7_
  64.9 0.0 collective-permute-done.8.refs_1_
  65.0 1.3 %collective-permute-done.9.refs_2_ = bf16[432,128]{1,0:T(8,128)(2,1)S(1)} collective-permute-done((bf16[432,128]{1,0:T(8,128)(2,1)S(1)}, bf16[432,128]{1,0:T(8,128)(2,1)S(1)}, u32[]{:S(2)}, u32[]{:S(2)}) %collective-permute-start.9) | collective-permute-done | bytes 110624 | tf_op jit(solution)/shard_map/ppermute | solution.py:409
  66.2 0.0 copy-done
  66.2 0.0 copy-done.1
  66.2 1.4 %home.1 = (bf16[128,1024]{1,0:T(8,128)(2,1)}, bf16[384,1024]{1,0:T(8,128)(2,1)}, f32[3,3,1024]{2,1,0:T(4,128)}) custom-call(s32[1]{0:T(128)} %bitcast.me_ref, bf16[432,128]{1,0:T(8,128)(2,1)S(1)} %get-tuple-element.36.refs_0_, bf16[432,128]{1,0:T(8,128)(2,1)S(1)} %collective-permute-done.8.refs_1_, bf16[432,128]{1,0:T(8,128)(2,1)S(1)} %collective-permute-done.9.refs_2_, ...), custom_call_target="tpu_custom_call" | custom-call | tf_op jit(solution)/shard_map/home/pallas_call | solution.py:514
  (1 shorter events, 0.0 us)
Async XLA Ops:
  2.2 19.8 %collective-permute-start = (bf16[640,128]{1,0:T(8,128)(2,1)S(1)}, bf16[640,128]{1,0:T(8,128)(2,1)S(1)}, u32[]{:S(2)}, u32[]{:S(2)}) collective-permute-start(bf16[640,128]{1,0:T(8,128)(2,1)S(1)} %get-tuple-element.25.packed_ref), channel_id=1, source_target_pairs={{0,8},{2,10},{4,12},{6,14},{8,0},{10,2},{12,4},{14,6},{1,9},{3,11}... | collective-permute-start | bytes 491528 | tf_op jit(solution)/shard_map/ppermute | solution.py:409
  6.3 20.4 %collective-permute-start.3 = (bf16[640,128]{1,0:T(8,128)(2,1)S(1)}, bf16[640,128]{1,0:T(8,128)(2,1)S(1)}, u32[]{:S(2)}, u32[]{:S(2)}) collective-permute-start(bf16[640,128]{1,0:T(8,128)(2,1)S(1)} %get-tuple-element.32), channel_id=1, source_target_pairs={{0,10},{2,8},{4,14},{6,12},{8,2},{10,0},{12,6},{14,4},{1,11},{3,9}... | collective-permute-start | bytes 491528 | tf_op jit(solution)/shard_map/ppermute | solution.py:409
  7.6 19.3 %collective-permute-start.4 = (bf16[640,128]{1,0:T(8,128)(2,1)S(1)}, bf16[640,128]{1,0:T(8,128)(2,1)S(1)}, u32[]{:S(2)}, u32[]{:S(2)}) collective-permute-start(bf16[640,128]{1,0:T(8,128)(2,1)S(1)} %get-tuple-element.33), channel_id=1, source_target_pairs={{0,12},{2,14},{4,8},{6,10},{8,4},{10,6},{12,0},{14,2},{1,13},{3,15... | collective-permute-start | bytes 491528 | tf_op jit(solution)/shard_map/ppermute | solution.py:409
  11.2 22.1 %collective-permute-start.1 = (bf16[768,128]{1,0:T(8,128)(2,1)S(1)}, bf16[768,128]{1,0:T(8,128)(2,1)S(1)}, u32[]{:S(2)}, u32[]{:S(2)}) collective-permute-start(bf16[768,128]{1,0:T(8,128)(2,1)S(1)} %get-tuple-element.30), channel_id=1, source_target_pairs={{0,6},{2,4},{4,2},{6,0},{8,14},{10,12},{12,10},{14,8},{1,7},{3,5},... | collective-permute-start | bytes 589832 | tf_op jit(solution)/shard_map/ppermute | solution.py:409
  11.2 23.6 %collective-permute-start.2 = (bf16[768,128]{1,0:T(8,128)(2,1)S(1)}, bf16[768,128]{1,0:T(8,128)(2,1)S(1)}, u32[]{:S(2)}, u32[]{:S(2)}) collective-permute-start(bf16[768,128]{1,0:T(8,128)(2,1)S(1)} %get-tuple-element.31), channel_id=1, source_target_pairs={{0,4},{2,6},{4,0},{6,2},{8,12},{10,14},{12,8},{14,10},{1,5},{3,7},... | collective-permute-start | bytes 589832 | tf_op jit(solution)/shard_map/ppermute | solution.py:409
  22.0 12.8 %collective-permute-start.5 = (bf16[768,128]{1,0:T(8,128)(2,1)S(1)}, bf16[768,128]{1,0:T(8,128)(2,1)S(1)}, u32[]{:S(2)}, u32[]{:S(2)}) collective-permute-start(bf16[768,128]{1,0:T(8,128)(2,1)S(1)} %get-tuple-element.34), channel_id=1, source_target_pairs={{0,14},{2,12},{4,10},{6,8},{8,6},{10,4},{12,2},{14,0},{1,15},{3,13... | collective-permute-start | bytes 589832 | tf_op jit(solution)/shard_map/ppermute | solution.py:409
  26.7 9.9 %collective-permute-start.6 = (bf16[768,128]{1,0:T(8,128)(2,1)S(1)}, bf16[768,128]{1,0:T(8,128)(2,1)S(1)}, u32[]{:S(2)}, u32[]{:S(2)}) collective-permute-start(bf16[768,128]{1,0:T(8,128)(2,1)S(1)} %get-tuple-element.35), channel_id=1, source_target_pairs={{0,2},{2,0},{4,6},{6,4},{8,10},{10,8},{12,14},{14,12},{1,3},{3,1},... | collective-permute-start | bytes 589832 | tf_op jit(solution)/shard_map/ppermute | solution.py:409
  26.9 9.7 %collective-permute-start.7 = (bf16[384,128]{1,0:T(8,128)(2,1)S(1)}, bf16[384,128]{1,0:T(8,128)(2,1)S(1)}, u32[]{:S(2)}, u32[]{:S(2)}) collective-permute-start(bf16[384,128]{1,0:T(8,128)(2,1)S(1)} %swap.1), channel_id=1, source_target_pairs={{0,16},{16,0},{1,17},{17,1},{2,18},{18,2},{3,19},{19,3},{4,20},{20... | collective-permute-start | bytes 294920 | tf_op jit(solution)/shard_map/ppermute | solution.py:511
  36.6 29.6 %copy-start = (bf16[16,8,1024]{2,1,0:T(8,128)(2,1)S(1)}, bf16[16,8,1024]{2,1,0:T(8,128)(2,1)}, u32[]{:S(2)}) copy-start(bf16[16,8,1024]{2,1,0:T(8,128)(2,1)} %param.9) | copy-start | bytes 786436
  36.6 29.6 %copy-start.1 = (f32[3,3,1024]{2,1,0:T(4,128)S(1)}, f32[3,3,1024]{2,1,0:T(4,128)}, u32[]{:S(2)}) copy-start(f32[3,3,1024]{2,1,0:T(4,128)} %refs_10_.1) | copy-start | bytes 110596
  46.0 10.7 %collective-permute-start.10 = (bf16[432,128]{1,0:T(8,128)(2,1)S(1)}, bf16[432,128]{1,0:T(8,128)(2,1)S(1)}, u32[]{:S(2)}, u32[]{:S(2)}) collective-permute-start(bf16[432,128]{1,0:T(8,128)(2,1)S(1)} %get-tuple-element.39), channel_id=1, source_target_pairs={{0,8},{2,10},{4,12},{6,14},{8,0},{10,2},{12,4},{14,6},{1,9},{3,11}... | collective-permute-start | bytes 331784 | tf_op jit(solution)/shard_map/ppermute | solution.py:409
  49.6 7.8 %collective-permute-start.11 = (bf16[432,128]{1,0:T(8,128)(2,1)S(1)}, bf16[432,128]{1,0:T(8,128)(2,1)S(1)}, u32[]{:S(2)}, u32[]{:S(2)}) collective-permute-start(bf16[432,128]{1,0:T(8,128)(2,1)S(1)} %get-tuple-element.40), channel_id=1, source_target_pairs={{0,6},{2,4},{4,2},{6,0},{8,14},{10,12},{12,10},{14,8},{1,7},{3,5},... | collective-permute-start | bytes 331784 | tf_op jit(solution)/shard_map/ppermute | solution.py:409
  49.6 15.3 %collective-permute-start.12 = (bf16[432,128]{1,0:T(8,128)(2,1)S(1)}, bf16[432,128]{1,0:T(8,128)(2,1)S(1)}, u32[]{:S(2)}, u32[]{:S(2)}) collective-permute-start(bf16[432,128]{1,0:T(8,128)(2,1)S(1)} %get-tuple-element.41), channel_id=1, source_target_pairs={{0,10},{2,8},{4,14},{6,12},{8,2},{10,0},{12,6},{14,4},{1,11},{3,9}... | collective-permute-start | bytes 331784 | tf_op jit(solution)/shard_map/ppermute | solution.py:409
  51.7 13.2 %collective-permute-start.13 = (bf16[432,128]{1,0:T(8,128)(2,1)S(1)}, bf16[432,128]{1,0:T(8,128)(2,1)S(1)}, u32[]{:S(2)}, u32[]{:S(2)}) collective-permute-start(bf16[432,128]{1,0:T(8,128)(2,1)S(1)} %get-tuple-element.42), channel_id=1, source_target_pairs={{0,14},{2,12},{4,10},{6,8},{8,6},{10,4},{12,2},{14,0},{1,15},{3,13... | collective-permute-start | bytes 331784 | tf_op jit(solution)/shard_map/ppermute | solution.py:409
  55.4 9.5 %collective-permute-start.14 = (bf16[432,128]{1,0:T(8,128)(2,1)S(1)}, bf16[432,128]{1,0:T(8,128)(2,1)S(1)}, u32[]{:S(2)}, u32[]{:S(2)}) collective-permute-start(bf16[432,128]{1,0:T(8,128)(2,1)S(1)} %get-tuple-element.43), channel_id=1, source_target_pairs={{0,12},{2,14},{4,8},{6,10},{8,4},{10,6},{12,0},{14,2},{1,13},{3,15... | collective-permute-start | bytes 331784 | tf_op jit(solution)/shard_map/ppermute | solution.py:409
  56.8 8.2 %collective-permute-start.8 = (bf16[432,128]{1,0:T(8,128)(2,1)S(1)}, bf16[432,128]{1,0:T(8,128)(2,1)S(1)}, u32[]{:S(2)}, u32[]{:S(2)}) collective-permute-start(bf16[432,128]{1,0:T(8,128)(2,1)S(1)} %get-tuple-element.37), channel_id=1, source_target_pairs={{0,2},{2,0},{4,6},{6,4},{8,10},{10,8},{12,14},{14,12},{1,3},{3,1},... | collective-permute-start | bytes 331784 | tf_op jit(solution)/shard_map/ppermute | solution.py:409
  57.4 8.8 %collective-permute-start.9 = (bf16[432,128]{1,0:T(8,128)(2,1)S(1)}, bf16[432,128]{1,0:T(8,128)(2,1)S(1)}, u32[]{:S(2)}, u32[]{:S(2)}) collective-permute-start(bf16[432,128]{1,0:T(8,128)(2,1)S(1)} %get-tuple-element.38), channel_id=1, source_target_pairs={{0,4},{2,6},{4,0},{6,2},{8,12},{10,14},{12,8},{14,10},{1,5},{3,7},... | collective-permute-start | bytes 331784 | tf_op jit(solution)/shard_map/ppermute | solution.py:409
